TPU v7x, 32 devices: a whole 2x2x4 slice. The times are simulated.
32 devices in a mesh: dp: 16 (over z, y, core), tensor: 2 (over x).
Axes of the slice: x: 2, y: 2, z: 4, core: 2. Of those that a mesh axis runs over, the one named last changes fastest.
Arguments:
- inputs: bfloat16 [32, 512, 768], P('dp'), may hold values from -6 to 6
- lengths: int32 [32], P('dp'), may hold values from 1 to 512, as said below
- w_qkv: bfloat16 [768, 3, 768], P(None, None, 'tensor'), may hold values from -0.21875 to 0.21875
- b_qv: float32 [2, 768], P(None, 'tensor'), may hold values from -3 to 3
- w_out: bfloat16 [768, 768], P('tensor'), may hold values from -0.875 to 0.875
- b_out: float32 [768], replicated, may hold values from -2 to 2
- ln_gains: float32 [2, 768], replicated, may hold values from 0.1 to 1.9
- ln_biases: float32 [2, 768], replicated, may hold values from -3 to 3
- w_in: bfloat16 [768, 3072], P(None, 'tensor'), may hold values from -0.21875 to 0.21875
- b_in: float32 [3072], P('tensor'), may hold values from -3 to 3
- w_down: bfloat16 [3072, 768], P('tensor'), may hold values from -0.109375 to 0.109375
- b_down: float32 [768], replicated, may hold values from -2 to 2
- cotangent: bfloat16 [32, 512, 768], P('dp'), may hold values from -6 to 6
Outputs:
- output: bfloat16 [32, 512, 768], P('dp')
- grad_inputs: float32 [32, 512, 768], P('dp')
- grad_w_qkv: float32 [768, 3, 768], P('dp', None, 'tensor')
- grad_b_qv: float32 [2, 768], P(None, 'tensor')
- grad_w_out: float32 [768, 768], P('tensor', 'dp')
- grad_b_out: float32 [768], replicated
- grad_ln_gains: float32 [2, 768], replicated
- grad_ln_biases: float32 [2, 768], replicated
- grad_w_in: float32 [768, 3072], P('dp', 'tensor')
- grad_b_in: float32 [3072], P('tensor')
- grad_w_down: float32 [3072, 768], P('tensor', 'dp')
- grad_b_down: float32 [768], replicated
Inputs may be any that keep to these rules, and one draw needn't show every extreme that they name: `lengths`: keys below this count are visible; in every draw some sequence has all 512.
All inputs are finite; a program needn't handle non-finite values.
Results may differ from a plain program's by a relative error of at most 0.012.
Values sent between devices are 32-bit elements; how exact they have to be, the bound alone decides.
No kernel may reach another device: no remote copies, remote signals or barrier semaphores. Data moves between devices by JAX's collectives and lax.ppermute only.
A program may use at most 128 MiB of HBM per device.

v0:
```python
import jax
import jax.numpy as jnp
from jax import lax
from jax.sharding import PartitionSpec as P

HEAD_DIM = 64
MICRO = 2


norm_eps = 1e-12
bfloat = jnp.bfloat16
single = jnp.float32


def normalize(hidden, gain_vec, offset):
    centred = hidden - jnp.mean(hidden, axis=-1, keepdims=True)
    second_moment = jnp.mean(centred * centred, axis=-1, keepdims=True)
    return centred * lax.rsqrt(second_moment + norm_eps) * gain_vec + offset


def gelu_exact(values):
    return jax.nn.gelu(values, approximate=False)


def contract_rows(left_side, right_side):
    return lax.dot_general(
        left_side, right_side, (((0,), (0,)), ((), ())), preferred_element_type=single
    )


def contract_cols(left_side, right_side):
    return lax.dot_general(
        left_side, right_side, (((1,), (1,)), ((), ())), preferred_element_type=single
    )


def masked_scores(queries, key_rows, visible):
    factor = queries.shape[-1] ** (-0.5)
    scores = jnp.einsum("qhd,khd->hqk", queries, key_rows, preferred_element_type=single) * factor
    return jnp.where(visible[None, None, :], scores, -1000000000.0)


def attend(queries, key_rows, value_rows, visible):
    scores = masked_scores(queries, key_rows, visible)
    highest = jnp.max(scores, axis=-1, keepdims=True)
    raised = jnp.exp(scores - highest)
    totals = jnp.sum(raised, axis=-1, keepdims=True)
    context = jnp.einsum(
        "hqk,khd->qhd", (raised / totals).astype(bfloat), value_rows, preferred_element_type=single
    )
    return (context.astype(bfloat), highest + jnp.log(totals))


def attend_back(queries, key_rows, value_rows, visible, log_total, grad_context):
    factor = queries.shape[-1] ** (-0.5)
    scores = masked_scores(queries, key_rows, visible)
    chances = jnp.exp(scores - log_total)
    grad_values = jnp.einsum(
        "hqk,qhd->khd", chances.astype(bfloat), grad_context, preferred_element_type=single
    )
    grad_chances = jnp.einsum(
        "qhd,khd->hqk", grad_context, value_rows, preferred_element_type=single
    )
    inner_sum = jnp.sum(chances * grad_chances, axis=-1, keepdims=True)
    grad_scores = (chances * (grad_chances - inner_sum)).astype(bfloat)
    grad_queries = (
        jnp.einsum("hqk,khd->qhd", grad_scores, key_rows, preferred_element_type=single) * factor
    )
    grad_keys = (
        jnp.einsum("hqk,qhd->khd", grad_scores, queries, preferred_element_type=single) * factor
    )
    return (grad_queries.astype(bfloat), grad_keys.astype(bfloat), grad_values.astype(bfloat))


def body(
    inputs,
    lengths,
    w_qkv,
    b_qv,
    w_out,
    b_out,
    ln_gains,
    ln_biases,
    w_in,
    b_in,
    w_down,
    b_down,
    cotangent,
):
    local_seqs, seq_len, model_width = inputs.shape
    per_micro = local_seqs // MICRO
    local_width = w_qkv.shape[2]
    heads_here = local_width // HEAD_DIM
    qkv_matrix = w_qkv.reshape(model_width, 3 * local_width)
    positions = jnp.arange(seq_len)
    head_shape = (per_micro, seq_len, heads_here, HEAD_DIM)
    outputs = []
    input_grads = []
    big_totals = None
    small_totals = None
    big_shares = None
    small_shares = None
    for micro_index in range(MICRO):
        first_seq = micro_index * per_micro
        batch_rows = inputs[first_seq : first_seq + per_micro].reshape(-1, model_width)
        batch_lengths = lengths[first_seq : first_seq + per_micro]
        visible = positions[None, :] < batch_lengths[:, None]
        projected = jnp.dot(batch_rows, qkv_matrix, preferred_element_type=single).reshape(
            -1, 3, local_width
        )
        queries = (projected[:, 0] + b_qv[0]).astype(bfloat).reshape(head_shape)
        key_rows = projected[:, 1].astype(bfloat).reshape(head_shape)
        value_rows = (projected[:, 2] + b_qv[1]).astype(bfloat).reshape(head_shape)
        context, log_total = lax.map(
            lambda packed: attend(*packed), (queries, key_rows, value_rows, visible)
        )
        context_rows = context.reshape(-1, local_width)
        attended = lax.psum(jnp.dot(context_rows, w_out, preferred_element_type=single), "tensor")
        normed_one, norm_one_back = jax.vjp(
            normalize, batch_rows.astype(single) + attended + b_out, ln_gains[0], ln_biases[0]
        )
        normed_low = normed_one.astype(bfloat)
        hidden_pre = jnp.dot(normed_low, w_in, preferred_element_type=single) + b_in
        hidden_act, gelu_back = jax.vjp(gelu_exact, hidden_pre)
        act_low = hidden_act.astype(bfloat)
        ffn_branch = lax.psum(jnp.dot(act_low, w_down, preferred_element_type=single), "tensor")
        normed_two, norm_two_back = jax.vjp(
            normalize, normed_one + ffn_branch + b_down, ln_gains[1], ln_biases[1]
        )
        outputs.append(normed_two.astype(bfloat).reshape(per_micro, seq_len, model_width))
        grad_out = (
            cotangent[first_seq : first_seq + per_micro].reshape(-1, model_width).astype(single)
        )
        grad_two, gain_two, shift_two = norm_two_back(grad_out)
        grad_branch = grad_two.astype(bfloat)
        (grad_hidden,) = gelu_back(contract_cols(grad_branch, w_down))
        grad_pre = grad_hidden.astype(bfloat)
        grad_normed = grad_two + lax.psum(contract_cols(grad_pre, w_in), "tensor")
        grad_one, gain_one, shift_one = norm_one_back(grad_normed)
        grad_attended = grad_one.astype(bfloat)
        grad_context = contract_cols(grad_attended, w_out).astype(bfloat).reshape(head_shape)
        grad_q, grad_k, grad_v = lax.map(
            lambda packed: attend_back(*packed),
            (queries, key_rows, value_rows, visible, log_total, grad_context),
        )
        grad_proj = jnp.stack(
            [
                grad_q.reshape(-1, local_width),
                grad_k.reshape(-1, local_width),
                grad_v.reshape(-1, local_width),
            ],
            axis=1,
        )
        grad_proj_flat = grad_proj.reshape(-1, 3 * local_width)
        input_part = lax.psum(contract_cols(grad_proj_flat, qkv_matrix), "tensor")
        input_grads.append((grad_one + input_part).reshape(per_micro, seq_len, model_width))
        big_pieces = (
            contract_rows(batch_rows, grad_proj_flat).reshape(model_width, 3, local_width),
            contract_rows(normed_low, grad_pre),
            contract_rows(context_rows, grad_attended),
            contract_rows(act_low, grad_branch),
        )
        small_pieces = (
            jnp.sum(grad_proj[:, 0::2].astype(single), axis=0),
            jnp.sum(grad_one, axis=0),
            jnp.stack([gain_one, gain_two]),
            jnp.stack([shift_one, shift_two]),
            jnp.sum(grad_pre.astype(single), axis=0),
            jnp.sum(grad_two, axis=0),
        )
        big_totals = (
            big_pieces
            if big_totals is None
            else tuple((older + newer for older, newer in zip(big_totals, big_pieces)))
        )
        small_totals = (
            small_pieces
            if small_totals is None
            else tuple((older + newer for older, newer in zip(small_totals, small_pieces)))
        )
    big_shares = (
        lax.psum_scatter(big_totals[0], "dp", scatter_dimension=0, tiled=True),
        lax.psum_scatter(big_totals[1], "dp", scatter_dimension=0, tiled=True),
        lax.psum_scatter(big_totals[2], "dp", scatter_dimension=1, tiled=True),
        lax.psum_scatter(big_totals[3], "dp", scatter_dimension=1, tiled=True),
    )
    small_shares = lax.psum(
        (
            small_totals[0],
            small_totals[1],
            small_totals[2],
            small_totals[3],
            small_totals[4],
            small_totals[5],
        ),
        "dp",
    )
    grad_qkv, grad_in, grad_out_w, grad_down = big_shares
    grad_bias_qv, grad_bias_out, grad_gains, grad_shifts, grad_bias_in, grad_bias_down = (
        small_shares
    )
    return (
        jnp.concatenate(outputs, axis=0),
        jnp.concatenate(input_grads, axis=0),
        grad_qkv,
        grad_bias_qv,
        grad_out_w,
        grad_bias_out,
        grad_gains,
        grad_shifts,
        grad_in,
        grad_bias_in,
        grad_down,
        grad_bias_down,
    )


def solution(mesh):
    placed = (
        P("dp", None, None),
        P("dp"),
        P(None, None, "tensor"),
        P(None, "tensor"),
        P("tensor", None),
        P(),
        P(),
        P(),
        P(None, "tensor"),
        P("tensor"),
        P("tensor", None),
        P(),
        P("dp", None, None),
    )
    return jax.shard_map(
        body,
        mesh=mesh,
        in_specs=placed,
        out_specs=(
            P("dp", None, None),
            P("dp", None, None),
            P("dp", None, "tensor"),
            P(None, "tensor"),
            P("tensor", "dp"),
            P(),
            P(),
            P(),
            P("dp", "tensor"),
            P("tensor"),
            P("tensor", "dp"),
            P(),
        ),
        check_vma=False,
    )
```

profile of v0, /device:TPU:0, one launch (start us, length us, event | category | flops | bytes accessed | tf_op | source)
XLA Modules:
  0.0 795.1 jit_solution(16959870812838222774)
XLA Ops:
  7.2 4.0 copy.40
  40.6 87.1 %all-reduce.16.cloned.1.call-done = (f32[512,768]{1,0:T(8,128)}, f32[512,768]{1,0:T(8,128)}) async-done(((f32[512,768]{1,0:T(8,128)}, f32[512,768]{1,0:T(8,128)}), (f32[512,768]{1,0:T(8,128)}, f32[512,768]{1,0:T(8,128)})) %all-reduce.16.cloned.1.call-update) | async-done | bytes 3145744 | tf_op jit(solution)/shard_map/psum | solution.py:118
  131.7 9.3 %multiply_convert_fusion.3 = (bf16[512,1536]{1,0:T(8,128)(2,1)S(1)}, f32[512,1536]{1,0:T(8,128)}, f32[512,1536]{1,0:T(8,128)}) fusion(f32[1536]{0:T(1024)S(1)} %copy-done.107, bf16[768,1536]{1,0:T(8,128)(2,1)S(1)} %copy-done, f32[512,768]{1,0:T(8,128)S(1)} %get-tuple-element.165, f32[768]{0:T(1024)S(1)} %copy-done.71, f32[768]{0:T(1024)S(1)} %get-tuple-element.209, ...), kind=kOutput, calls=%fused_computation.47 | convolution fusion | flops 1261830144 | bytes 11812864 | tf_op jit(solution)/shard_map/dot_general | solution.py:123
  141.1 9.3 %multiply_convert_fusion.2 = (bf16[512,1536]{1,0:T(8,128)(2,1)S(1)}, f32[512,1536]{1,0:T(8,128)}, f32[512,1536]{1,0:T(8,128)}) fusion(f32[1536]{0:T(1024)S(1)} %copy-done.107, bf16[768,1536]{1,0:T(8,128)(2,1)S(1)} %copy-done, f32[512,768]{1,0:T(8,128)S(1)} %get-tuple-element.180, f32[512]{0:T(512)S(1)} %fusion.69, f32[512]{0:T(512)S(1)} %broadcast_multiply_fusion.1, ...), kind=kOutput, calls=%fused_computation.34 | convolution fusion | flops 1261830144 | bytes 11812864 | tf_op jit(solution)/shard_map/dot_general | solution.py:123
  156.0 85.6 %all-reduce.14.cloned.1.call-done = (f32[512,768]{1,0:T(8,128)}, f32[512,768]{1,0:T(8,128)}) async-done(((f32[512,768]{1,0:T(8,128)}, f32[512,768]{1,0:T(8,128)}), (f32[512,768]{1,0:T(8,128)}, f32[512,768]{1,0:T(8,128)})) %all-reduce.14.cloned.1.call-update) | async-done | bytes 3145744 | tf_op jit(solution)/shard_map/psum | solution.py:126
  241.6 3.9 fusion.84
  270.4 83.3 %all-reduce.12.cloned.1.call-done = (f32[512,768]{1,0:T(8,128)}, f32[512,768]{1,0:T(8,128)}) async-done(((f32[512,768]{1,0:T(8,128)}, f32[512,768]{1,0:T(8,128)}), (f32[512,768]{1,0:T(8,128)}, f32[512,768]{1,0:T(8,128)})) %all-reduce.12.cloned.1.call-update) | async-done | bytes 3145744 | tf_op jit(solution)/shard_map/psum | solution.py:138
  353.8 4.0 multiply_reduce_fusion.2
  357.9 4.9 multiply_reduce_fusion.3
  367.2 4.0 multiply_reduce_fusion.1
  371.2 4.8 multiply_convert_fusion.1
  383.0 4.1 multiply_reduce_fusion
  387.1 4.6 multiply_convert_fusion
  402.9 4.2 convolution_bitcast_fusion.1
  414.8 4.2 fusion.77
  419.0 3.8 convolution_add_fusion.2
  427.2 3.8 convolution_add_fusion.1
  445.2 5.2 copy.57
  455.3 40.3 %all-reduce.10.cloned.1.call-done = (f32[512,768]{1,0:T(8,128)}, f32[512,768]{1,0:T(8,128)}) async-done(((f32[512,768]{1,0:T(8,128)}, f32[512,768]{1,0:T(8,128)}), (f32[512,768]{1,0:T(8,128)}, f32[512,768]{1,0:T(8,128)})) %all-reduce.10.cloned.1.call-update) | async-done | bytes 3145744 | tf_op jit(solution)/shard_map/psum | solution.py:155
  500.5 62.0 %all-reduce = (f32[2,384]{1,0:T(2,128)}, f32[768]{0:T(1024)}, f32[2,768]{1,0:T(2,128)}, f32[2,768]{1,0:T(2,128)}, f32[1536]{0:T(1024)}, /*index=5*/f32[768]{0:T(1024)}) all-reduce(f32[2,384]{1,0:T(2,128)S(1)} %add.314, f32[768]{0:T(1024)S(1)} %add.316, ...), channel_id=1, replica_groups=mesh['dp'=16,'tensor'=2] {'dp'}, use_global_device_ids=true, to_apply=%region_33.34 | all-reduce | flops 6912 | bytes 55296 | tf_op jit(solution)/shard_map/psum | solution.py:187
  562.5 3.7 pad_maximum_fusion
  566.3 70.5 %reduce-scatter.9.cloned.1.call-done = f32[48,1536]{1,0:T(8,128)} async-done(((f32[768,1536]{1,0:T(8,128)}), f32[48,1536]{1,0:T(8,128)}) %reduce-scatter.9.cloned.1.call-update) | async-done | bytes 294928 | tf_op jit(solution)/shard_map/reduce_scatter | solution.py:183
  636.8 79.5 %reduce-scatter.11.cloned.1.call-done = f32[1536,48]{0,1:T(8,128)} async-done(((f32[1536,768]{0,1:T(8,128)}), f32[1536,48]{0,1:T(8,128)}) %reduce-scatter.11.cloned.1.call-update) | async-done | bytes 294928 | tf_op jit(solution)/shard_map/reduce_scatter | solution.py:185
  716.3 71.6 %reduce-scatter.5.cloned.1.call-done = f32[48,3,384]{2,0,1:T(8,128)} async-done(((f32[768,3,384]{2,0,1:T(8,128)}), f32[48,3,384]{2,0,1:T(8,128)}) %reduce-scatter.5.cloned.1.call-update) | async-done | bytes 221200 | tf_op jit(solution)/shard_map/reduce_scatter | solution.py:182
  (349 shorter events, 121.1 us)
Async XLA Ops:
  7.2 124.5 %copy-start = (bf16[768,1536]{1,0:T(8,128)(2,1)S(1)}, bf16[768,1536]{1,0:T(8,128)(2,1)}, u32[]{:S(2)}) copy-start(bf16[768,1536]{1,0:T(8,128)(2,1)} %param.21) | copy-start | bytes 7077892
  7.2 120.5 %all-reduce.16.cloned.1.call-start = ((), (), s32[]{:S(2)}) async-start(), calls=%async_computation.11 | async-start | bytes 6291456 | tf_op jit(solution)/shard_map/psum | solution.py:118
  22.0 11.4 %copy-start.69 = (f32[6,64]{1,0:T(8,128)}, f32[6,64]{1,0:T(8,128)S(1)}, u32[]{:S(2)}) copy-start(f32[6,64]{1,0:T(8,128)S(1)} %add.272) | copy-start | bytes 4612
  37.1 90.6 %copy-start.102 = (f32[768]{0:T(1024)S(1)}, f32[768]{0:T(1024)}, u32[]{:S(2)}) copy-start(f32[768]{0:T(1024)} %param.18) | copy-start | bytes 9220
  38.9 202.7 %all-reduce.14.cloned.1.call-start = ((), (), s32[]{:S(2)}) async-start(), calls=%async_computation.10 | async-start | bytes 6291456 | tf_op jit(solution)/shard_map/psum | solution.py:126
  40.6 201.0 %copy-start.50 = (f32[768]{0:T(1024)}, f32[768]{0:T(1024)S(1)}, u32[]{:S(2)}) copy-start(f32[768]{0:T(1024)S(1)} %get-tuple-element.209) | copy-start | bytes 9220
  130.6 10.5 %copy-start.3 = (f32[512,768]{1,0:T(8,128)}, f32[512,768]{1,0:T(8,128)S(1)}, u32[]{:S(2)}) copy-start(f32[512,768]{1,0:T(8,128)S(1)} %get-tuple-element.180) | copy-start | bytes 4718596
  130.6 10.5 %copy-start.6 = (f32[512,768]{1,0:T(8,128)}, f32[512,768]{1,0:T(8,128)S(1)}, u32[]{:S(2)}) copy-start(f32[512,768]{1,0:T(8,128)S(1)} %get-tuple-element.165) | copy-start | bytes 4718596
  130.6 111.0 %copy-start.63 = (f32[512]{0:T(512)}, f32[512]{0:T(512)S(1)}, u32[]{:S(2)}) copy-start(f32[512]{0:T(512)S(1)} %broadcast_multiply_fusion.3) | copy-start | bytes 6148
  130.7 111.0 %copy-start.58 = (f32[512]{0:T(512)}, f32[512]{0:T(512)S(1)}, u32[]{:S(2)}) copy-start(f32[512]{0:T(512)S(1)} %broadcast_multiply_fusion.1) | copy-start | bytes 6148
  131.1 9.9 %copy-start.83 = (f32[512]{0:T(512)}, f32[512]{0:T(512)S(1)}, u32[]{:S(2)}) copy-start(f32[512]{0:T(512)S(1)} %get-tuple-element.208) | copy-start | bytes 6148
  131.7 110.0 %copy-start.66 = (f32[512]{0:T(512)}, f32[512]{0:T(512)S(1)}, u32[]{:S(2)}) copy-start(f32[512]{0:T(512)S(1)} %fusion.69) | copy-start | bytes 6148
  131.7 9.4 %copy-start.74 = (f32[512]{0:T(512)}, f32[512]{0:T(512)S(1)}, u32[]{:S(2)}) copy-start(f32[512]{0:T(512)S(1)} %fusion.67) | copy-start | bytes 6148
  141.1 9.4 %copy-start.29 = (bf16[512,1536]{1,0:T(8,128)(2,1)}, bf16[512,1536]{1,0:T(8,128)(2,1)S(1)}, u32[]{:S(2)}) copy-start(bf16[512,1536]{1,0:T(8,128)(2,1)S(1)} %get-tuple-element.162) | copy-start | bytes 4718596
  155.5 198.2 %all-reduce.12.cloned.1.call-start = ((), (), s32[]{:S(2)}) async-start(), calls=%async_computation.9 | async-start | bytes 6291456 | tf_op jit(solution)/shard_map/psum | solution.py:138
  267.6 228.1 %all-reduce.10.cloned.1.call-start = ((), (), s32[]{:S(2)}) async-start(), calls=%async_computation.8 | async-start | bytes 6291456 | tf_op jit(solution)/shard_map/psum | solution.py:155
  353.8 11.5 %slice-start.2 = ((s8[6291456]{0:T(1024)(128)(4,1)}), s8[4194304]{0:T(1024)(128)(4,1)S(1)}, s32[]{:S(2)}) async-start(s8[6291456]{0:T(1024)(128)(4,1)} %bitcast.152), calls=%async_computation.14 | async-start | bytes 8388608
  371.2 9.9 %slice-start = ((s8[6291456]{0:T(1024)(128)(4,1)}), s8[4194304]{0:T(1024)(128)(4,1)S(1)}, s32[]{:S(2)}) async-start(s8[6291456]{0:T(1024)(128)(4,1)} %bitcast.150), calls=%async_computation.12 | async-start | bytes 8388608
  371.2 9.9 %slice-start.1 = ((s8[6291456]{0:T(1024)(128)(4,1)}), s8[2097152]{0:T(1024)(128)(4,1)S(1)}, s32[]{:S(2)}) async-start(s8[6291456]{0:T(1024)(128)(4,1)} %bitcast.150), calls=%async_computation.13 | async-start | bytes 4194304
  395.2 12.0 %copy-start.38 = (bf16[512,1,384]{2,0,1:T(8,128)(2,1)}, bf16[512,1,384]{2,0,1:T(8,128)(2,1)S(1)}, u32[]{:S(2)}) copy-start(bf16[512,1,384]{2,0,1:T(8,128)(2,1)S(1)} %copy.54) | copy-start | bytes 1179652
  409.6 156.7 %reduce-scatter.7.cloned.1.call-start = ((), (), s32[]{:S(2)}) async-start(), calls=%async_computation.5 | async-start | bytes 1253376 | tf_op jit(solution)/shard_map/reduce_scatter | solution.py:184
  414.7 222.1 %reduce-scatter.9.cloned.1.call-start = ((), (), s32[]{:S(2)}) async-start(), calls=%async_computation.6 | async-start | bytes 5013504 | tf_op jit(solution)/shard_map/reduce_scatter | solution.py:183
  422.9 293.4 %reduce-scatter.11.cloned.1.call-start = ((), (), s32[]{:S(2)}) async-start(), calls=%async_computation.7 | async-start | bytes 5013504 | tf_op jit(solution)/shard_map/reduce_scatter | solution.py:185
  431.0 356.9 %reduce-scatter.5.cloned.1.call-start = ((), (), s32[]{:S(2)}) async-start(), calls=%async_computation.4 | async-start | bytes 3760128 | tf_op jit(solution)/shard_map/reduce_scatter | solution.py:182
  (101 other events, 318.0 us)
Sparse Core Ops, SparseCore 0:
  39.0 88.6 all-reduce.15
  155.6 85.9 all-reduce.13
  267.7 85.9 all-reduce.11
  409.7 85.9 all-reduce.9
  499.7 58.1 reduce-scatter.6
  562.2 74.5 reduce-scatter.8
  641.7 74.5 reduce-scatter.10
  720.7 67.0 reduce-scatter.4
where the time goes:
time: 804 us; the launch traced here: 795 us
  waiting for transfers between devices  518 us (64%)
  matrix products  101 us (13%)
  blocking collectives  62 us (8%)
  other arithmetic  53.7 us (7%)
  local copies, waits for them, and re-layouts  43.3 us (5%)
  between operations  16 us (2%)
    psum x1, waiting for transfers between devices, body(): lax.psum(jnp.dot(context_rows, w_out, preferred_element_type=single), 'te...  87.1 us
    psum x1, waiting for transfers between devices, body(): lax.psum(jnp.dot(act_low, w_down, preferred_element_type=single), 'tensor')  85.6 us
    psum x1, waiting for transfers between devices, body(): grad_normed = grad_two + lax.psum(contract_cols(grad_pre, w_in), 'tensor')  83.3 us
    reduce_scatter x1, waiting for transfers between devices, body(): lax.psum_scatter(big_totals[3], 'dp', scatter_dimension=1, tiled=True)  79.5 us
    reduce_scatter x1, waiting for transfers between devices, body(): lax.psum_scatter(big_totals[0], 'dp', scatter_dimension=0, tiled=True)  71.6 us
    reduce_scatter x1, waiting for transfers between devices, body(): lax.psum_scatter(big_totals[1], 'dp', scatter_dimension=0, tiled=True)  70.5 us
    psum x1, blocking collectives, body(): lax.psum((small_totals[0], small_totals[1], small_totals[2], small_totals...  62 us
    psum x1, waiting for transfers between devices, body(): input_part = lax.psum(contract_cols(grad_proj_flat, qkv_matrix), 'tensor')  40.3 us
  transfers between devices with their start and end apart: 8, of which 7 were waited for; matrix products, arithmetic and copies ran while one was open for 7% of the time, Pallas kernels for 0%

commit v1 on v0

v1 whole, which is shorter than its diff:
```python
import functools

import jax
import jax.numpy as jnp
from jax import lax
from jax.experimental import pallas as pl
from jax.experimental.pallas import tpu as pltpu
from jax.sharding import PartitionSpec as P

HEAD_DIM = 64
norm_eps = 1e-12
bfloat = jnp.bfloat16
single = jnp.float32


def dot(left, right):
    return jnp.dot(left, right, preferred_element_type=single)


def dot_rows(left, right):
    return lax.dot_general(
        left, right, (((0,), (0,)), ((), ())), preferred_element_type=single
    )


def dot_cols(left, right):
    return lax.dot_general(
        left, right, (((1,), (1,)), ((), ())), preferred_element_type=single
    )


def swap_dp(value, mask, size):
    return lax.ppermute(value, "dp", [(i, i ^ mask) for i in range(size)])


def swap_x(value):
    return lax.ppermute(value, "tensor", [(0, 1), (1, 0)])


def reverse_bits(position, bits):
    out = 0
    for k in range(bits):
        out |= ((position >> k) & 1) << (bits - 1 - k)
    return out


def place_kernel(order_ref, block_ref, out_ref):
    out_ref[...] = block_ref[...].astype(out_ref.dtype)


def place(blocks, order):
    count, rows, width = blocks.shape
    return pl.pallas_call(
        place_kernel,
        grid_spec=pltpu.PrefetchScalarGridSpec(
            num_scalar_prefetch=1,
            grid=(count,),
            in_specs=[pl.BlockSpec((1, rows, width), lambda p, order: (p, 0, 0))],
            out_specs=pl.BlockSpec((1, rows, width), lambda p, order: (order[p], 0, 0)),
        ),
        out_shape=jax.ShapeDtypeStruct((count, rows, width), bfloat),
    )(order, blocks).reshape(count * rows, width)


def fetch_spread(own, me, size):
    bits = min(size, 16).bit_length() - 1
    count = 1 << bits
    rank = me % count
    rows = own.shape[0] // count
    held = lax.dynamic_slice_in_dim(own, rank * rows, rows).astype(single)
    held = swap_x(held)
    for k in reversed(range(1, bits)):
        held = jnp.concatenate([held, swap_dp(held, 1 << k, size)], axis=0)
    held = jnp.concatenate([held, swap_dp(held, 1, size)], axis=0)
    order = jnp.array([reverse_bits(p, bits) for p in range(count)], jnp.int32) ^ rank
    return place(held.reshape(count, rows, own.shape[1]), order)


def fetch_direct(own, me, size):
    rows = own.shape[0] // 2
    core = me % 2
    held = swap_x(lax.dynamic_slice_in_dim(own, core * rows, rows).astype(single))
    held = jnp.stack([held, swap_dp(held, 1, size)])
    return place(held, jnp.arange(2, dtype=jnp.int32) ^ core)


def halve(value, mask, size):
    middle = value.shape[0] // 2
    return value[:middle] + swap_dp(value[middle:], mask, size)


def scatter_sum(left_rel, own_side, other_side, size, x_first):
    middle = left_rel.shape[1] // 2
    keep, send = left_rel[:, :middle], left_rel[:, middle:]
    other_in = swap_dp(dot_rows(send, other_side), 1, size)
    own_in = swap_dp(dot_rows(send, own_side), 1, size)
    other = dot_rows(keep, other_side) + other_in
    own = dot_rows(keep, own_side) + own_in
    masks = [1 << k for k in range(1, size.bit_length() - 1)]
    if x_first:
        total = own + swap_x(other)
        for mask in masks:
            total = halve(total, mask, size)
        return total
    for mask in masks:
        other = halve(other, mask, size)
        own = halve(own, mask, size)
    return own + swap_x(other)


def sum_all(value, size):
    for k in range(size.bit_length() - 1):
        value = value + swap_dp(value, 1 << k, size)
    return value


def norm_parts(hidden):
    centred = hidden - jnp.mean(hidden, axis=-1, keepdims=True)
    scale = lax.rsqrt(jnp.mean(centred * centred, axis=-1, keepdims=True) + norm_eps)
    return centred * scale, scale


def norm_back(upstream, unit, scale, gain):
    scaled = upstream * gain
    return scale * (
        scaled
        - jnp.mean(scaled, axis=-1, keepdims=True)
        - unit * jnp.mean(scaled * unit, axis=-1, keepdims=True)
    )


def split_heads(rows):
    return rows.reshape(rows.shape[0], -1, HEAD_DIM)


def masked_scores(queries, keys, visible):
    scores = jnp.einsum("qhd,khd->hqk", queries, keys, preferred_element_type=single)
    return jnp.where(visible[None, None, :], scores * HEAD_DIM**-0.5, -1e9)


def attend(queries, keys, values, visible):
    queries, keys, values = map(split_heads, (queries, keys, values))
    scores = masked_scores(queries, keys, visible)
    highest = jnp.max(scores, axis=-1, keepdims=True)
    raised = jnp.exp(scores - highest)
    totals = jnp.sum(raised, axis=-1, keepdims=True)
    context = jnp.einsum(
        "hqk,khd->qhd", (raised / totals).astype(bfloat), values, preferred_element_type=single
    )
    return context.astype(bfloat).reshape(context.shape[0], -1), highest + jnp.log(totals)


def attend_back(queries, keys, values, visible, log_total, grad_context):
    queries, keys, values, grad_context = map(
        split_heads, (queries, keys, values, grad_context)
    )
    chances = jnp.exp(masked_scores(queries, keys, visible) - log_total)
    grad_values = jnp.einsum(
        "hqk,qhd->khd", chances.astype(bfloat), grad_context, preferred_element_type=single
    )
    grad_chances = jnp.einsum(
        "qhd,khd->hqk", grad_context, values, preferred_element_type=single
    )
    inner = jnp.sum(chances * grad_chances, axis=-1, keepdims=True)
    grad_scores = (chances * (grad_chances - inner)).astype(bfloat)
    factor = HEAD_DIM**-0.5
    grad_queries = factor * jnp.einsum(
        "hqk,khd->qhd", grad_scores, keys, preferred_element_type=single
    )
    grad_keys = factor * jnp.einsum(
        "hqk,qhd->khd", grad_scores, queries, preferred_element_type=single
    )
    return tuple(
        part.astype(bfloat).reshape(part.shape[0], -1)
        for part in (grad_queries, grad_keys, grad_values)
    )


def body(
    inputs,
    lengths,
    w_qkv,
    b_qv,
    w_out,
    b_out,
    ln_gains,
    ln_biases,
    w_in,
    b_in,
    w_down,
    b_down,
    cotangent,
):
    size = lax.axis_size("dp")
    me = lax.axis_index("dp")
    side = lax.axis_index("tensor")
    width = inputs.shape[2]
    local = w_qkv.shape[2]
    rows = lax.dynamic_index_in_dim(inputs, side, 0, keepdims=False)
    length = lax.dynamic_index_in_dim(lengths, side, 0, keepdims=False)
    upstream = lax.dynamic_index_in_dim(cotangent, side, 0, keepdims=False)
    visible = jnp.arange(rows.shape[0]) < length

    qkv_own = w_qkv.reshape(width, 3 * local)
    middle = w_down.shape[0] // 2
    small_other = swap_x(jnp.concatenate([b_qv.reshape(-1), b_in]))
    b_qv_other, b_in_other = small_other[: 2 * local].reshape(2, local), small_other[2 * local :]
    qkv_other = fetch_spread(qkv_own, me, size)
    out_other = fetch_direct(w_out, me, size)
    in_other = fetch_spread(w_in, me, size)
    down_other = jnp.concatenate(
        [fetch_spread(w_down[:middle], me, size), fetch_direct(w_down[middle:], me, size)]
    )
    sides = (
        (qkv_own, b_qv, w_out, w_in, b_in, w_down),
        (qkv_other, b_qv_other, out_other, in_other, b_in_other, down_other),
    )

    bits = size.bit_length() - 1
    share = width // size
    block_of = jnp.array([reverse_bits(p, bits) for p in range(size)], jnp.int32) ^ me
    source = (block_of[:, None] * share + jnp.arange(share)[None, :]).reshape(-1)
    reorder = (jnp.arange(width)[:, None] == source[None, :]).astype(bfloat)

    def relative(value):
        return dot(value, reorder).astype(bfloat)

    heads = []
    hidden = rows.astype(single) + b_out
    for qkv, bias, out, _, _, _ in sides:
        projected = dot(rows, qkv)
        queries = (projected[:, :local] + bias[0]).astype(bfloat)
        keys = projected[:, local : 2 * local].astype(bfloat)
        values = (projected[:, 2 * local :] + bias[1]).astype(bfloat)
        context, log_total = attend(queries, keys, values, visible)
        hidden = hidden + dot(context, out)
        heads.append((queries, keys, values, log_total, context))
    unit_one, scale_one = norm_parts(hidden)
    normed = unit_one * ln_gains[0] + ln_biases[0]
    normed_low = normed.astype(bfloat)
    hidden_two = normed + b_down
    acts = []
    for _, _, _, into, bias, down in sides:
        pre = dot(normed_low, into) + bias
        chance = 0.5 * (1.0 + lax.erf(pre * 0.7071067811865476))
        act = (pre * chance).astype(bfloat)
        slope = chance + pre * jnp.exp(-0.5 * pre * pre) * 0.3989422804014327
        hidden_two = hidden_two + dot(act, down)
        acts.append((act, slope))
    unit_two, scale_two = norm_parts(hidden_two)
    result = unit_two * ln_gains[1] + ln_biases[1]
    result_other = swap_x(unit_two) * ln_gains[1] + ln_biases[1]

    upstream = upstream.astype(single)
    grad_two = norm_back(upstream, unit_two, scale_two, ln_gains[1])
    branch = grad_two.astype(bfloat)
    branch_rel = relative(branch)
    normed_rel = relative(normed_low)
    rows_rel = relative(rows)
    share_down = scatter_sum(branch_rel, acts[0][0], acts[1][0], size, True)
    grad_pres = []
    grad_normed = grad_two
    for (_, slope), (_, _, _, into, _, down) in zip(acts, sides):
        grad_pre = (dot_cols(branch, down) * slope).astype(bfloat)
        grad_normed = grad_normed + dot_cols(grad_pre, into)
        grad_pres.append(grad_pre)
    share_in = scatter_sum(normed_rel, grad_pres[0], grad_pres[1], size, False)
    grad_one = norm_back(grad_normed, unit_one, scale_one, ln_gains[0])
    attended = grad_one.astype(bfloat)
    attended_rel = relative(attended)
    share_out = scatter_sum(attended_rel, heads[0][4], heads[1][4], size, False)
    grad_rows = grad_one
    grad_projs = []
    for (queries, keys, values, log_total, _), (qkv, _, out, _, _, _) in zip(heads, sides):
        grad_context = dot_cols(attended, out).astype(bfloat)
        parts = attend_back(queries, keys, values, visible, log_total, grad_context)
        grad_proj = jnp.concatenate(parts, axis=1)
        grad_rows = grad_rows + dot_cols(grad_proj, qkv)
        grad_projs.append(grad_proj)
    grad_rows_other = swap_x(grad_rows)
    share_qkv = scatter_sum(rows_rel, grad_projs[0], grad_projs[1], size, True)

    def columns(value):
        return jnp.sum(value.astype(single), axis=0)

    every = jnp.concatenate(
        [
            columns(grad_one),
            columns(grad_normed * unit_one),
            columns(upstream * unit_two),
            columns(grad_normed),
            columns(upstream),
            columns(grad_two),
        ]
    )
    vectors = jnp.concatenate([every, columns(grad_pres[0])])
    vectors_other = swap_x(jnp.concatenate([every, columns(grad_pres[1])]))
    vectors = sum_all(vectors + vectors_other, size)
    low_part, high_part = grad_projs[0], grad_projs[1]
    qv_own = jnp.concatenate([columns(low_part[:, :local]), columns(low_part[:, 2 * local :])])
    qv_other = jnp.concatenate([columns(high_part[:, :local]), columns(high_part[:, 2 * local :])])
    grad_b_qv = sum_all(qv_own + swap_x(qv_other), size).reshape(2, local)
    b_out_g, gain_one, gain_two, shift_one, shift_two, b_down_g = (
        vectors[k * width : (k + 1) * width] for k in range(6)
    )

    def both(mine, other):
        mine, other = mine[None], other[None]
        return jnp.where(
            side == 0,
            jnp.concatenate([mine, other], axis=0),
            jnp.concatenate([other, mine], axis=0),
        )

    return (
        both(result.astype(bfloat), result_other.astype(bfloat)),
        both(grad_rows, grad_rows_other),
        share_qkv.reshape(-1, 3, local),
        grad_b_qv,
        share_out.T,
        b_out_g,
        jnp.stack([gain_one, gain_two]),
        jnp.stack([shift_one, shift_two]),
        share_in,
        vectors[6 * width :],
        share_down.T,
        b_down_g,
    )


def solution(mesh):
    placed = (
        P("dp", None, None),
        P("dp"),
        P(None, None, "tensor"),
        P(None, "tensor"),
        P("tensor", None),
        P(),
        P(),
        P(),
        P(None, "tensor"),
        P("tensor"),
        P("tensor", None),
        P(),
        P("dp", None, None),
    )
    return jax.shard_map(
        body,
        mesh=mesh,
        in_specs=placed,
        out_specs=(
            P("dp", None, None),
            P("dp", None, None),
            P("dp", None, "tensor"),
            P(None, "tensor"),
            P("tensor", "dp"),
            P(),
            P(),
            P(),
            P("dp", "tensor"),
            P("tensor"),
            P("tensor", "dp"),
            P(),
        ),
        check_vma=False,
    )
```

time: 804 us -> 596 us (0.74)
  waiting for transfers between devices: 518 us -> 314 us
  blocking collectives: 62 us -> 0 us
  starting transfers between devices: 0.95 us -> 52.1 us
  Pallas kernels: 0 us -> 37.2 us
  between operations: 16 us -> 2.74 us
  other arithmetic: 53.7 us -> 43.8 us
    ppermute x0 -> x62, waiting for transfers between devices: none -> 314 us  [the longest x48 175 us: swap_dp(): return lax.ppermute(value, 'dp', [(i, i ^ mask) for i in range(size)])]
    psum x4 -> x0, waiting for transfers between devices: 296 us -> none  [the longest x1 87.1 us: body(): lax.psum(jnp.dot(context_rows, w_out, preferred_element_type=single), 'te...]
    reduce_scatter x4 -> x0, waiting for transfers between devices: 222 us -> none  [the longest x1 79.5 us: body(): lax.psum_scatter(big_totals[3], 'dp', scatter_dimension=1, tiled=True)]
    psum x1 -> x0, blocking collectives: 62 us -> none  [body(): lax.psum((small_totals[0], small_totals[1], small_totals[2], small_totals...]
    ppermute x0 -> x62, starting transfers between devices: none -> 52.1 us  [the longest x48 35.5 us: swap_dp(): return lax.ppermute(value, 'dp', [(i, i ^ mask) for i in range(size)])]
    pallas_call x0 -> x5, Pallas kernels: none -> 37.2 us  [place(): pl.pallas_call(place_kernel, grid_spec=pltpu.PrefetchScalarGridSpec(num_s...]
    reduce_sum x15 -> x6, other arithmetic: 28.6 us -> 6.95 us  [the longest x4 6.36 us: columns(): return jnp.sum(value.astype(single), axis=0)]
    another operation x8 -> x4, local copies, waits for them, and re-layouts: 12.1 us -> 0.01 us  [the longest x2 0.01 us: body(): jnp.stack([gain_one, gain_two])]
  transfers between devices with their start and end apart: 8 -> 62, of which waited for: 7 -> 26; matrix products, arithmetic and copies ran while one was open for 7% -> 17% of each run, Pallas kernels for 0% -> 5%
where the time goes in v1:
time: 596 us; the launch traced here: 587 us
  waiting for transfers between devices  314 us (53%)
  matrix products  98.5 us (17%)
  starting transfers between devices  52.1 us (9%)
  other arithmetic  43.8 us (7%)
  local copies, waits for them, and re-layouts  39 us (7%)
  Pallas kernels  37.2 us (6%)
    ppermute x48, waiting for transfers between devices, swap_dp(): return lax.ppermute(value, 'dp', [(i, i ^ mask) for i in range(size)])  175 us
    ppermute x14, waiting for transfers between devices, swap_x(): return lax.ppermute(value, 'tensor', [(0, 1), (1, 0)])  139 us
    pallas_call x5, Pallas kernels, place(): pl.pallas_call(place_kernel, grid_spec=pltpu.PrefetchScalarGridSpec(num_s...  37.2 us
    ppermute x48, starting transfers between devices, swap_dp(): return lax.ppermute(value, 'dp', [(i, i ^ mask) for i in range(size)])  35.5 us
    dot_general x16, matrix products, dot_rows(): lax.dot_general(left, right, (((0,), (0,)), ((), ())), preferred_element_...  28 us
    dot_general x12, matrix products, dot(): return jnp.dot(left, right, preferred_element_type=single)  26 us
    dot_general x8, matrix products, dot_cols(): lax.dot_general(left, right, (((1,), (1,)), ((), ())), preferred_element_...  24.7 us
    unnamed x240, local copies, waits for them, and re-layouts  21.6 us
  transfers between devices with their start and end apart: 62, of which 26 were waited for; matrix products, arithmetic and copies ran while one was open for 17% of the time, Pallas kernels for 5%

profile of v1, /device:TPU:0, one launch (start us, length us, event | category | flops | bytes accessed | tf_op | source)
XLA Modules:
  0.0 587.0 jit_solution(13624778870957682839)
XLA Ops:
  31.2 31.2 %collective-permute-done.13 = f32[48,768]{1,0:T(8,128)S(1)} collective-permute-done((f32[48,768]{1,0:T(8,128)S(1)}, f32[48,768]{1,0:T(8,128)S(1)}, u32[]{:S(2)}, u32[]{:S(2)}) %collective-permute-start.13) | collective-permute-done | bytes 147488 | tf_op jit(solution)/shard_map/ppermute | solution.py:37
  66.7 10.1 %collective-permute-done.14 = f32[48,768]{1,0:T(8,128)S(1)} collective-permute-done((f32[48,768]{1,0:T(8,128)S(1)}, f32[48,768]{1,0:T(8,128)S(1)}, u32[]{:S(2)}, u32[]{:S(2)}) %collective-permute-start.14) | collective-permute-done | bytes 147488 | tf_op jit(solution)/shard_map/ppermute | solution.py:33
  82.1 10.5 %collective-permute-done.9 = f32[48,1536]{1,0:T(8,128)S(1)} collective-permute-done((f32[48,1536]{1,0:T(8,128)S(1)}, f32[48,1536]{1,0:T(8,128)S(1)}, u32[]{:S(2)}, u32[]{:S(2)}) %collective-permute-start.9) | collective-permute-done | bytes 294944 | tf_op jit(solution)/shard_map/ppermute | solution.py:33
  94.1 8.4 %collective-permute-done.2 = f32[96,1152]{1,0:T(8,128)S(1)} collective-permute-done((f32[96,1152]{1,0:T(8,128)S(1)}, f32[96,1152]{1,0:T(8,128)S(1)}, u32[]{:S(2)}, u32[]{:S(2)}) %collective-permute-start.2) | collective-permute-done | bytes 442400 | tf_op jit(solution)/shard_map/ppermute | solution.py:33
  107.1 8.0 %collective-permute-done.10 = f32[96,1536]{1,0:T(8,128)S(1)} collective-permute-done((f32[96,1536]{1,0:T(8,128)S(1)}, f32[96,1536]{1,0:T(8,128)S(1)}, u32[]{:S(2)}, u32[]{:S(2)}) %collective-permute-start.10) | collective-permute-done | bytes 589856 | tf_op jit(solution)/shard_map/ppermute | solution.py:33
  117.7 7.5 %collective-permute-done.3 = f32[192,1152]{1,0:T(8,128)S(1)} collective-permute-done((f32[192,1152]{1,0:T(8,128)S(1)}, f32[192,1152]{1,0:T(8,128)S(1)}, u32[]{:S(2)}, u32[]{:S(2)}) %collective-permute-start.3) | collective-permute-done | bytes 884768 | tf_op jit(solution)/shard_map/ppermute | solution.py:33
  126.7 11.1 %collective-permute-done.16 = f32[192,768]{1,0:T(8,128)S(1)} collective-permute-done((f32[192,768]{1,0:T(8,128)S(1)}, f32[192,768]{1,0:T(8,128)S(1)}, u32[]{:S(2)}, u32[]{:S(2)}) %collective-permute-start.16) | collective-permute-done | bytes 589856 | tf_op jit(solution)/shard_map/ppermute | solution.py:33
  146.7 15.5 %collective-permute-done.11 = f32[192,1536]{1,0:T(8,128)} collective-permute-done((f32[192,1536]{1,0:T(8,128)}, f32[192,1536]{1,0:T(8,128)}, u32[]{:S(2)}, u32[]{:S(2)}) %collective-permute-start.11) | collective-permute-done | bytes 1179680 | tf_op jit(solution)/shard_map/ppermute | solution.py:33
  173.9 10.0 %shard_map.259 = bf16[16,48,768]{2,1,0:T(8,128)(2,1)} custom-call(s32[16]{0:T(128)} %get-tuple-element.107.order_ref, f32[16,48,768]{2,1,0:T(8,128)} %bitcast.172), custom_call_target="tpu_custom_call" | custom-call | tf_op jit(solution)/shard_map/pallas_call | solution.py:53
  189.1 10.7 %shard_map.256 = bf16[16,48,1152]{2,1,0:T(8,128)(2,1)} custom-call(s32[16]{0:T(128)} %get-tuple-element.107.order_ref, f32[16,48,1152]{2,1,0:T(8,128)} %bitcast.8.block_ref), custom_call_target="tpu_custom_call" | custom-call | tf_op jit(solution)/shard_map/pallas_call | solution.py:53
  220.3 10.6 %shard_map.258 = bf16[16,48,1536]{2,1,0:T(8,128)(2,1)} custom-call(s32[16]{0:T(128)} %get-tuple-element.107.order_ref, f32[16,48,1536]{2,1,0:T(8,128)} %bitcast.18.block_ref), custom_call_target="tpu_custom_call" | custom-call | tf_op jit(solution)/shard_map/pallas_call | solution.py:53
  231.0 4.7 multiply_convert_fusion.2
  245.8 30.1 %collective-permute-done.20 = f32[512,768]{1,0:T(8,128)} collective-permute-done((f32[512,768]{1,0:T(8,128)S(1)}, f32[512,768]{1,0:T(8,128)}, u32[]{:S(2)}, u32[]{:S(2)}) %collective-permute-start.20) | collective-permute-done | bytes 1572896 | tf_op jit(solution)/shard_map/ppermute | solution.py:37
  279.1 4.7 convert_reduce_fusion
  283.8 11.4 %convert_reduce_fusion.1 = (f32[1536]{0:T(1024)}, bf16[512,1536]{1,0:T(8,128)(2,1)S(1)}) fusion(f32[512,1536]{1,0:T(8,128)S(1)} %copy-done.103, bf16[1536,768]{1,0:T(8,128)(2,1)S(1)} %copy-done.47, f32[512,768]{1,0:T(8,128)S(1)} %get-tuple-element.74), kind=kOutput, calls=%fused_computation.37 | convolution fusion | flops 1217788416 | bytes 8656896 | tf_op jit(solution)/shard_map/dot_general | solution.py:27
  306.7 4.8 multiply_convert_fusion.1
  373.2 6.5 %collective-permute-done.38 = f32[192,384]{1,0:T(8,128)S(1)} collective-permute-done((f32[192,384]{1,0:T(8,128)S(1)}, f32[192,384]{1,0:T(8,128)S(1)}, u32[]{:S(2)}, u32[]{:S(2)}) %collective-permute-start.38) | collective-permute-done | bytes 294944 | tf_op jit(solution)/shard_map/ppermute | solution.py:33
  381.5 7.1 %collective-permute-done.34 = f32[192,384]{1,0:T(8,128)S(1)} collective-permute-done((f32[192,384]{1,0:T(8,128)S(1)}, f32[192,384]{1,0:T(8,128)S(1)}, u32[]{:S(2)}, u32[]{:S(2)}) %collective-permute-start.34) | collective-permute-done | bytes 294944 | tf_op jit(solution)/shard_map/ppermute | solution.py:33
  417.9 53.3 %collective-permute-done.41 = f32[48,384]{1,0:T(8,128)S(1)} collective-permute-done((f32[48,384]{1,0:T(8,128)S(1)}, f32[48,384]{1,0:T(8,128)S(1)}, u32[]{:S(2)}, u32[]{:S(2)}) %collective-permute-start.41) | collective-permute-done | bytes 73760 | tf_op jit(solution)/shard_map/ppermute | solution.py:37
  479.5 20.6 %collective-permute-done.48 = f32[192,1536]{1,0:T(8,128)S(1)} collective-permute-done((f32[192,1536]{1,0:T(8,128)S(1)}, f32[192,1536]{1,0:T(8,128)S(1)}, u32[]{:S(2)}, u32[]{:S(2)}) %collective-permute-start.48) | collective-permute-done | bytes 1179680 | tf_op jit(solution)/shard_map/ppermute | solution.py:33
  503.0 22.1 %collective-permute-done.58 = f32[384,1536]{1,0:T(8,128)S(1)} collective-permute-done((f32[384,1536]{1,0:T(8,128)S(1)}, f32[384,1536]{1,0:T(8,128)S(1)}, u32[]{:S(2)}, u32[]{:S(2)}) %collective-permute-start.58) | collective-permute-done | bytes 2359328 | tf_op jit(solution)/shard_map/ppermute | solution.py:37
  532.1 21.2 %collective-permute-done.59 = f32[192,1536]{1,0:T(8,128)S(1)} collective-permute-done((f32[192,1536]{1,0:T(8,128)S(1)}, f32[192,1536]{1,0:T(8,128)S(1)}, u32[]{:S(2)}, u32[]{:S(2)}) %collective-permute-start.59) | collective-permute-done | bytes 1179680 | tf_op jit(solution)/shard_map/ppermute | solution.py:33
  556.8 15.1 %collective-permute-done.60 = f32[96,1536]{1,0:T(8,128)S(1)} collective-permute-done((f32[96,1536]{1,0:T(8,128)S(1)}, f32[96,1536]{1,0:T(8,128)S(1)}, u32[]{:S(2)}, u32[]{:S(2)}) %collective-permute-start.60) | collective-permute-done | bytes 589856 | tf_op jit(solution)/shard_map/ppermute | solution.py:33
  572.8 13.0 %collective-permute-done.61 = f32[48,1536]{1,0:T(8,128)S(1)} collective-permute-done((f32[48,1536]{1,0:T(8,128)S(1)}, f32[48,1536]{1,0:T(8,128)S(1)}, u32[]{:S(2)}, u32[]{:S(2)}) %collective-permute-start.61) | collective-permute-done | bytes 294944 | tf_op jit(solution)/shard_map/ppermute | solution.py:33
  (526 shorter events, 236.4 us)
Async XLA Ops:
  8.1 57.6 %collective-permute-start = (f32[48,1152]{1,0:T(8,128)S(1)}, f32[48,1152]{1,0:T(8,128)S(1)}, u32[]{:S(2)}, u32[]{:S(2)}) collective-permute-start(f32[48,1152]{1,0:T(8,128)S(1)} %convert_element_type.178), channel_id=1, source_target_pairs={{0,1},{1,0},{2,3},{3,2},{4,5},{5,4},{6,7},{7,6},{8,9},{9,8},{10,11... | collective-permute-start | bytes 663560 | tf_op jit(solution)/shard_map/ppermute | solution.py:37
  9.1 95.8 %collective-permute-start.6 = (f32[192,768]{1,0:T(8,128)}, f32[192,768]{1,0:T(8,128)}, u32[]{:S(2)}, u32[]{:S(2)}) collective-permute-start(f32[192,768]{1,0:T(8,128)} %dynamic-slice_convert_fusion.1), channel_id=1, source_target_pairs={{0,1},{1,0},{2,3},{3,2},{4,5},{5,4},{6,7},{7,6},{8,9},{9,8},{10,11... | collective-permute-start | bytes 1769480 | tf_op jit(solution)/shard_map/ppermute | solution.py:37
  12.0 64.9 %collective-permute-start.8 = (f32[48,1536]{1,0:T(8,128)S(1)}, f32[48,1536]{1,0:T(8,128)S(1)}, u32[]{:S(2)}, u32[]{:S(2)}) collective-permute-start(f32[48,1536]{1,0:T(8,128)S(1)} %dynamic-slice_convert_fusion.2), channel_id=1, source_target_pairs={{0,1},{1,0},{2,3},{3,2},{4,5},{5,4},{6,7},{7,6},{8,9},{9,8},{10,11... | collective-permute-start | bytes 884744 | tf_op jit(solution)/shard_map/ppermute | solution.py:37
  16.0 101.7 %collective-permute-start.18 = (f32[384,768]{1,0:T(8,128)}, f32[384,768]{1,0:T(8,128)}, u32[]{:S(2)}, u32[]{:S(2)}) collective-permute-start(f32[384,768]{1,0:T(8,128)} %dynamic-slice_convert_fusion), channel_id=1, source_target_pairs={{0,1},{1,0},{2,3},{3,2},{4,5},{5,4},{6,7},{7,6},{8,9},{9,8},{10,11... | collective-permute-start | bytes 3538952 | tf_op jit(solution)/shard_map/ppermute | solution.py:37
  104.3 33.6 %collective-permute-start.16 = (f32[192,768]{1,0:T(8,128)S(1)}, f32[192,768]{1,0:T(8,128)S(1)}, u32[]{:S(2)}, u32[]{:S(2)}) collective-permute-start(f32[192,768]{1,0:T(8,128)S(1)} %pad_maximum_fusion.15), channel_id=1, source_target_pairs={{0,4},{2,6},{4,0},{6,2},{8,12},{10,14},{12,8},{14,10},{16,20},{18,... | collective-permute-start | bytes 1769480 | tf_op jit(solution)/shard_map/ppermute | solution.py:33
  104.8 34.3 %collective-permute-start.7 = (f32[192,768]{1,0:T(8,128)}, f32[192,768]{1,0:T(8,128)S(1)}, u32[]{:S(2)}, u32[]{:S(2)}) collective-permute-start(f32[192,768]{1,0:T(8,128)} %collective-permute-done.6), channel_id=1, source_target_pairs={{0,2},{2,0},{4,6},{6,4},{8,10},{10,8},{12,14},{14,12},{16,18},{18,... | collective-permute-start | bytes 1769480 | tf_op jit(solution)/shard_map/ppermute | solution.py:33
  116.2 46.0 %collective-permute-start.11 = (f32[192,1536]{1,0:T(8,128)}, f32[192,1536]{1,0:T(8,128)}, u32[]{:S(2)}, u32[]{:S(2)}) collective-permute-start(f32[192,1536]{1,0:T(8,128)} %pad_maximum_fusion.9), channel_id=1, source_target_pairs={{0,4},{2,6},{4,0},{6,2},{8,12},{10,14},{12,8},{14,10},{16,20},{18,... | collective-permute-start | bytes 3538952 | tf_op jit(solution)/shard_map/ppermute | solution.py:33
  117.7 47.3 %collective-permute-start.19 = (f32[384,768]{1,0:T(8,128)}, f32[384,768]{1,0:T(8,128)}, u32[]{:S(2)}, u32[]{:S(2)}) collective-permute-start(f32[384,768]{1,0:T(8,128)} %collective-permute-done.18), channel_id=1, source_target_pairs={{0,2},{2,0},{4,6},{6,4},{8,10},{10,8},{12,14},{14,12},{16,18},{18,... | collective-permute-start | bytes 3538952 | tf_op jit(solution)/shard_map/ppermute | solution.py:33
  126.7 59.6 %collective-permute-start.4 = (f32[384,1152]{1,0:T(8,128)}, f32[384,1152]{1,0:T(8,128)}, u32[]{:S(2)}, u32[]{:S(2)}) collective-permute-start(f32[384,1152]{1,0:T(8,128)} %pad_maximum_fusion.3), channel_id=1, source_target_pairs={{0,2},{2,0},{4,6},{6,4},{8,10},{10,8},{12,14},{14,12},{16,18},{18,... | collective-permute-start | bytes 5308424 | tf_op jit(solution)/shard_map/ppermute | solution.py:33
  139.1 32.5 %collective-permute-start.17 = (f32[384,768]{1,0:T(8,128)}, f32[384,768]{1,0:T(8,128)}, u32[]{:S(2)}, u32[]{:S(2)}) collective-permute-start(f32[384,768]{1,0:T(8,128)} %pad_maximum_fusion.10), channel_id=1, source_target_pairs={{0,2},{2,0},{4,6},{6,4},{8,10},{10,8},{12,14},{14,12},{16,18},{18,... | collective-permute-start | bytes 3538952 | tf_op jit(solution)/shard_map/ppermute | solution.py:33
  165.0 52.1 %collective-permute-start.12 = (f32[384,1536]{1,0:T(8,128)}, f32[384,1536]{1,0:T(8,128)}, u32[]{:S(2)}, u32[]{:S(2)}) collective-permute-start(f32[384,1536]{1,0:T(8,128)} %pad_maximum_fusion), channel_id=1, source_target_pairs={{0,2},{2,0},{4,6},{6,4},{8,10},{10,8},{12,14},{14,12},{16,18},{18,... | collective-permute-start | bytes 7077896 | tf_op jit(solution)/shard_map/ppermute | solution.py:33
  239.0 36.9 %collective-permute-start.20 = (f32[512,768]{1,0:T(8,128)S(1)}, f32[512,768]{1,0:T(8,128)}, u32[]{:S(2)}, u32[]{:S(2)}) collective-permute-start(f32[512,768]{1,0:T(8,128)S(1)} %get-tuple-element.77), channel_id=1, source_target_pairs={{0,1},{1,0},{2,3},{3,2},{4,5},{5,4},{6,7},{7,6},{8,9},{9,8},{10,11... | collective-permute-start | bytes 4718600 | tf_op jit(solution)/shard_map/ppermute | solution.py:37
  353.7 46.7 %collective-permute-start.51 = (f32[384,1536]{1,0:T(8,128)}, f32[384,1536]{1,0:T(8,128)}, u32[]{:S(2)}, u32[]{:S(2)}) collective-permute-start(f32[384,1536]{1,0:T(8,128)} %fusion.79), channel_id=1, source_target_pairs={{0,2},{2,0},{4,6},{6,4},{8,10},{10,8},{12,14},{14,12},{16,18},{18,... | collective-permute-start | bytes 7077896 | tf_op jit(solution)/shard_map/ppermute | solution.py:33
  357.6 50.3 %collective-permute-start.23 = (f32[384,1152]{1,0:T(8,128)}, f32[384,1152]{1,0:T(8,128)}, u32[]{:S(2)}, u32[]{:S(2)}) collective-permute-start(f32[384,1152]{1,0:T(8,128)} %fusion.91), channel_id=1, source_target_pairs={{0,2},{2,0},{4,6},{6,4},{8,10},{10,8},{12,14},{14,12},{16,18},{18,... | collective-permute-start | bytes 5308424 | tf_op jit(solution)/shard_map/ppermute | solution.py:33
  367.1 47.0 %collective-permute-start.47 = (f32[384,1536]{1,0:T(8,128)}, f32[384,1536]{1,0:T(8,128)S(1)}, u32[]{:S(2)}, u32[]{:S(2)}) collective-permute-start(f32[384,1536]{1,0:T(8,128)} %fusion.81), channel_id=1, source_target_pairs={{0,2},{2,0},{4,6},{6,4},{8,10},{10,8},{12,14},{14,12},{16,18},{18,... | collective-permute-start | bytes 7077896 | tf_op jit(solution)/shard_map/ppermute | solution.py:33
  371.1 44.5 %collective-permute-start.57 = (f32[384,1536]{1,0:T(8,128)S(1)}, f32[384,1536]{1,0:T(8,128)S(1)}, u32[]{:S(2)}, u32[]{:S(2)}) collective-permute-start(f32[384,1536]{1,0:T(8,128)S(1)} %copy-done.21), channel_id=1, source_target_pairs={{0,2},{2,0},{4,6},{6,4},{8,10},{10,8},{12,14},{14,12},{16,18},{18,... | collective-permute-start | bytes 7077896 | tf_op jit(solution)/shard_map/ppermute | solution.py:33
  398.9 72.3 %collective-permute-start.21 = (f32[512,768]{1,0:T(8,128)S(1)}, f32[512,768]{1,0:T(8,128)S(1)}, u32[]{:S(2)}, u32[]{:S(2)}) collective-permute-start(f32[512,768]{1,0:T(8,128)S(1)} %copy-done.59), channel_id=1, source_target_pairs={{0,1},{1,0},{2,3},{3,2},{4,5},{5,4},{6,7},{7,6},{8,9},{9,8},{10,11... | collective-permute-start | bytes 4718600 | tf_op jit(solution)/shard_map/ppermute | solution.py:37
  407.9 63.8 %collective-permute-start.52 = (f32[192,1536]{1,0:T(8,128)S(1)}, f32[192,1536]{1,0:T(8,128)S(1)}, u32[]{:S(2)}, u32[]{:S(2)}) collective-permute-start(f32[192,1536]{1,0:T(8,128)S(1)} %slice.328), channel_id=1, source_target_pairs={{0,4},{2,6},{4,0},{6,2},{8,12},{10,14},{12,8},{14,10},{16,20},{18,... | collective-permute-start | bytes 3538952 | tf_op jit(solution)/shard_map/ppermute | solution.py:33
  414.1 61.9 %collective-permute-start.22 = (f32[384,1152]{1,0:T(8,128)S(1)}, f32[384,1152]{1,0:T(8,128)S(1)}, u32[]{:S(2)}, u32[]{:S(2)}) collective-permute-start(f32[384,1152]{1,0:T(8,128)S(1)} %copy-done.99), channel_id=1, source_target_pairs={{0,2},{2,0},{4,6},{6,4},{8,10},{10,8},{12,14},{14,12},{16,18},{18,... | collective-permute-start | bytes 5308424 | tf_op jit(solution)/shard_map/ppermute | solution.py:33
  414.1 63.5 %collective-permute-start.24 = (f32[384,1152]{1,0:T(8,128)S(1)}, f32[384,1152]{1,0:T(8,128)S(1)}, u32[]{:S(2)}, u32[]{:S(2)}) collective-permute-start(f32[384,1152]{1,0:T(8,128)S(1)} %convolution_add_fusion.2), channel_id=1, source_target_pairs={{0,1},{1,0},{2,3},{3,2},{4,5},{5,4},{6,7},{7,6},{8,9},{9,8},{10,11... | collective-permute-start | bytes 5308424 | tf_op jit(solution)/shard_map/ppermute | solution.py:37
  415.6 55.6 %collective-permute-start.41 = (f32[48,384]{1,0:T(8,128)S(1)}, f32[48,384]{1,0:T(8,128)S(1)}, u32[]{:S(2)}, u32[]{:S(2)}) collective-permute-start(f32[48,384]{1,0:T(8,128)S(1)} %slice_add_fusion.20), channel_id=1, source_target_pairs={{0,1},{1,0},{2,3},{3,2},{4,5},{5,4},{6,7},{7,6},{8,9},{9,8},{10,11... | collective-permute-start | bytes 221192 | tf_op jit(solution)/shard_map/ppermute | solution.py:37
  471.2 31.7 %collective-permute-start.56 = (f32[384,1536]{1,0:T(8,128)S(1)}, f32[384,1536]{1,0:T(8,128)S(1)}, u32[]{:S(2)}, u32[]{:S(2)}) collective-permute-start(f32[384,1536]{1,0:T(8,128)S(1)} %copy-done.20), channel_id=1, source_target_pairs={{0,2},{2,0},{4,6},{6,4},{8,10},{10,8},{12,14},{14,12},{16,18},{18,... | collective-permute-start | bytes 7077896 | tf_op jit(solution)/shard_map/ppermute | solution.py:33
  471.7 53.3 %collective-permute-start.58 = (f32[384,1536]{1,0:T(8,128)S(1)}, f32[384,1536]{1,0:T(8,128)S(1)}, u32[]{:S(2)}, u32[]{:S(2)}) collective-permute-start(f32[384,1536]{1,0:T(8,128)S(1)} %convolution_add_fusion.4), channel_id=1, source_target_pairs={{0,1},{1,0},{2,3},{3,2},{4,5},{5,4},{6,7},{7,6},{8,9},{9,8},{10,11... | collective-permute-start | bytes 7077896 | tf_op jit(solution)/shard_map/ppermute | solution.py:37
  478.4 50.2 %collective-permute-start.25 = (f32[192,1152]{1,0:T(8,128)S(1)}, f32[192,1152]{1,0:T(8,128)S(1)}, u32[]{:S(2)}, u32[]{:S(2)}) collective-permute-start(f32[192,1152]{1,0:T(8,128)S(1)} %slice.295), channel_id=1, source_target_pairs={{0,4},{2,6},{4,0},{6,2},{8,12},{10,14},{12,8},{14,10},{16,20},{18,... | collective-permute-start | bytes 2654216 | tf_op jit(solution)/shard_map/ppermute | solution.py:33
  (148 other events, 1337.0 us)

commit v2 on v1

v2 whole, which is shorter than its diff:
```python
import functools

import jax
import jax.numpy as jnp
from jax import lax
from jax.experimental import pallas as pl
from jax.experimental.pallas import tpu as pltpu
from jax.sharding import PartitionSpec as P

HEAD_DIM = 64
PAIR = 2 * HEAD_DIM
norm_eps = 1e-12
bfloat = jnp.bfloat16
single = jnp.float32
MIB = 1 << 20


def dot(left, right):
    return jnp.dot(left, right, preferred_element_type=single)


def dot_cols(left, right):
    return lax.dot_general(
        left, right, (((1,), (1,)), ((), ())), preferred_element_type=single
    )


def shaped(shape, dtype):
    return jax.ShapeDtypeStruct(shape, dtype)


def call(kernel, outs, *args, scalars=(), scratch=(), grid=(), in_specs=None, out_specs=None, limit=48):
    many = isinstance(outs, (tuple, list))
    if in_specs is None:
        in_specs = [pl.BlockSpec(memory_space=pltpu.VMEM)] * len(args)
        out_specs = [pl.BlockSpec(memory_space=pltpu.VMEM)] * len(outs) if many else pl.BlockSpec(memory_space=pltpu.VMEM)
    return pl.pallas_call(
        kernel,
        out_shape=outs,
        grid=grid,
        in_specs=[pl.BlockSpec(memory_space=pltpu.SMEM)] * len(scalars) + list(in_specs),
        out_specs=out_specs,
        scratch_shapes=list(scratch),
        compiler_params=pltpu.CompilerParams(vmem_limit_bytes=limit * MIB),
        cost_estimate=pl.CostEstimate(flops=1000, bytes_accessed=1000, transcendentals=0),
    )(*scalars, *args)


def swap_dp(value, mask, size):
    return lax.ppermute(value, "dp", [(i, i ^ mask) for i in range(size)])


def swap_x(value):
    return lax.ppermute(value, "tensor", [(0, 1), (1, 0)])


def reverse_bits(position, bits):
    out = 0
    for k in range(bits):
        out |= ((position >> k) & 1) << (bits - 1 - k)
    return out


def place_kernel(groups, rows, order_ref, *refs):
    out_ref = refs[-1]
    at = 0
    for piece, count in zip(refs[:-1], groups):
        for b in range(count):
            start = pl.multiple_of(order_ref[at], 16)
            height = rows[at]
            if out_ref.ndim == 3:
                out_ref[:, pl.ds(start, height), :] = piece[b].astype(out_ref.dtype)
            else:
                out_ref[pl.ds(start, height), :] = piece[b].astype(out_ref.dtype)
            at += 1


def place(parts, shape):
    pieces, rows, starts = [], [], []
    for held, begin in parts:
        pieces += held
        starts += begin
        rows += [held[0].shape[-2]] * len(begin)
    groups = tuple(piece.shape[0] for piece in pieces)
    kernel = functools.partial(place_kernel, groups, tuple(rows))
    return call(kernel, shaped(shape, bfloat), *pieces, scalars=(jnp.stack(starts),))


def fetch_spread(own, me, size, masks, base=0):
    masks = [mask for mask in masks if mask < size]
    count = 2 << len(masks)
    rank = me & (count - 1)
    rows = own.shape[-2] // count
    held = lax.dynamic_slice_in_dim(own, rank * rows, rows, axis=own.ndim - 2).astype(single)
    pieces = [swap_x(held)[None]]
    offsets = [[0]]
    for mask in masks:
        whole = pieces[0] if len(pieces) == 1 else jnp.concatenate(pieces, axis=0)
        flat = [o for part in offsets for o in part]
        pieces = [whole, swap_dp(whole, mask, size)]
        offsets = [flat, [o ^ mask for o in flat]]
    pieces = pieces + [swap_dp(piece, 1, size) for piece in pieces]
    flat = [o for part in offsets for o in part]
    flat = flat + [o ^ 1 for o in flat]
    return pieces, [base + (rank ^ o) * rows for o in flat]


def fetch_direct(own, me, size, base=0):
    rows = own.shape[0] // 2
    core = me & 1
    held = swap_x(lax.dynamic_slice_in_dim(own, core * rows, rows).astype(single))[None]
    return [held, swap_dp(held, 1, size)], [base + core * rows, base + (1 - core) * rows]


def halve(value, mask, size):
    middle = value.shape[-2] // 2
    return value[..., :middle, :] + swap_dp(value[..., middle:, :], mask, size)


def sum_all(value, size):
    for k in range(size.bit_length() - 1):
        value = value + swap_dp(value, 1 << k, size)
    return value


def grad_kernel(sides, terms, split, *refs):
    left_ref = refs[0]
    rights = refs[1 : 1 + sides]
    added = refs[1 + sides : 1 + sides + terms]
    outs = refs[1 + sides + terms :]

    def step(right_ref):
        total = dot(left_ref[...], right_ref[...])
        for term in added:
            total = total + term[...].reshape(total.shape)
        if split:
            middle = total.shape[0] // 2
            outs[0][...] = total[:middle].reshape(outs[0].shape)
            outs[1][...] = total[middle:].reshape(outs[1].shape)
        else:
            outs[0][...] = total.reshape(outs[0].shape)

    if sides == 1:
        step(rights[0])
    else:
        pl.when(pl.program_id(0) == 0)(lambda: step(rights[0]))
        pl.when(pl.program_id(0) == 1)(lambda: step(rights[1]))


def grad_part(left, half, rights, added=(), split=False):
    depth, tokens = left.shape
    rows = depth // 2
    width = rights[0].shape[1]
    tile = 512 if width % 512 == 0 else 384
    steps = width // tile
    sides = len(rights)
    if sides == 1:
        grid = (steps,)
        right_specs = [pl.BlockSpec((tokens, tile), lambda j: (0, j))]
        left_spec = pl.BlockSpec((rows, tokens), lambda j: (half, 0))

        def block(height):
            return pl.BlockSpec((height, tile), lambda j: (0, j))

        def full(height):
            return (height, width)
    else:
        grid = (2, steps)
        right_specs = [
            pl.BlockSpec((tokens, tile), lambda s, j: (0, jnp.where(s == 0, j, steps - 1))),
            pl.BlockSpec((tokens, tile), lambda s, j: (0, jnp.where(s == 0, 0, j))),
        ]
        left_spec = pl.BlockSpec((rows, tokens), lambda s, j: (half, 0))

        def block(height):
            return pl.BlockSpec((1, height, tile), lambda s, j: (s, 0, j))

        def full(height):
            return (2, height, width)

    heights = (rows // 2, rows // 2) if split else (rows,)
    outs = call(
        functools.partial(grad_kernel, sides, len(added), split),
        [shaped(full(height), single) for height in heights],
        left,
        *rights,
        *added,
        grid=grid,
        in_specs=[left_spec, *right_specs, *[block(rows) for _ in added]],
        out_specs=[block(height) for height in heights],
        limit=32,
    )
    return outs if split else outs[0]


def finish(low, high, size):
    total = low + swap_dp(high, 2, size)
    for k in range(2, size.bit_length() - 1):
        total = halve(total, 1 << k, size)
    return total


def scatter_x_first(left, own, other, size):
    other_in = swap_dp(grad_part(left, 1, [other]), 1, size)
    own_in = swap_dp(grad_part(left, 1, [own]), 1, size)
    across = swap_x(grad_part(left, 0, [other], [other_in]))
    low, high = grad_part(left, 0, [own], [own_in, across], split=True)
    return finish(low, high, size)


def scatter_y_first(left, own, other, size):
    arrived = swap_dp(grad_part(left, 1, [own, other]), 1, size)
    low, high = grad_part(left, 0, [own, other], [arrived], split=True)
    total = finish(low, high, size)
    return total[0] + swap_x(total[1])


def relative_kernel(value_ref, source_ref, out_ref):
    depth = value_ref.shape[1]
    tile = depth // 4

    def step(j, carry):
        at = pl.multiple_of(j * tile, 16)
        lanes = lax.broadcasted_iota(jnp.int32, (tile, depth), 1)
        picks = jnp.where(lanes == source_ref[pl.ds(at, tile), :], 1.0, 0.0).astype(bfloat)
        out_ref[pl.ds(at, tile), :] = dot_cols(picks, value_ref[...]).astype(bfloat)
        return carry

    lax.fori_loop(0, 4, step, 0)


def relative(value, source):
    return call(relative_kernel, shaped(value.shape[::-1], bfloat), value, source)


def attend_kernel(length_ref, rows_ref, qkv_ref, bias_ref, out_w_ref, start_ref, parts_ref, chance_ref, context_ref, hidden_ref, turned_ref):
    tokens = rows_ref.shape[0]
    local = qkv_ref.shape[2]
    rows = rows_ref[...]
    for part in range(3):
        projected = dot(rows, qkv_ref[part])
        if part == 0:
            projected = projected + bias_ref[0:1, :]
        elif part == 2:
            projected = projected + bias_ref[1:2, :]
        parts_ref[part] = projected.astype(bfloat)
    tile = 256
    visible = lax.broadcasted_iota(jnp.int32, (tokens, tile), 0) < length_ref[0]

    def pair_step(pair, carry):
        at = pl.multiple_of(pair * PAIR, PAIR)
        keys = parts_ref[1, :, pl.ds(at, PAIR)]
        queries = parts_ref[0, :, pl.ds(at, PAIR)].T
        values = parts_ref[2, :, pl.ds(at, PAIR)].T
        owner = lax.broadcasted_iota(jnp.int32, (PAIR, tile), 0) // HEAD_DIM
        for h in range(2):
            value_rows = values[h * HEAD_DIM : (h + 1) * HEAD_DIM]
            for q in range(tokens // tile):
                picked = queries[:, q * tile : (q + 1) * tile] * HEAD_DIM**-0.5
                picked = jnp.where(owner == h, picked, jnp.zeros_like(picked))
                scores = jnp.where(visible, dot(keys, picked), -1e9)
                raised = jnp.exp(scores - jnp.max(scores, axis=0, keepdims=True))
                chances = raised * (1.0 / jnp.sum(raised, axis=0, keepdims=True))
                chances = chances.astype(bfloat)
                chance_ref[pair * 2 + h, :, q * tile : (q + 1) * tile] = chances
                turned_ref[pl.ds(pl.multiple_of(at + h * HEAD_DIM, HEAD_DIM), HEAD_DIM), q * tile : (q + 1) * tile] = dot(value_rows, chances).astype(bfloat)
        return carry

    lax.fori_loop(0, local // PAIR, pair_step, 0)
    context = turned_ref[...].T
    context_ref[...] = context
    hidden_ref[...] = start_ref[...] + dot(context, out_w_ref[...])


def attend(length, rows, qkv, bias, out, start):
    tokens, width = rows.shape
    local = qkv.shape[2]
    return call(
        attend_kernel,
        [
            shaped((3, tokens, local), bfloat),
            shaped((local // HEAD_DIM, tokens, tokens), bfloat),
            shaped((tokens, local), bfloat),
            shaped((tokens, width), single),
        ],
        rows,
        qkv,
        bias,
        out,
        start,
        scalars=(length,),
        scratch=[pltpu.VMEM((local, tokens), bfloat)],
    )


def unit_of(hidden):
    centred = hidden - jnp.mean(hidden, axis=-1, keepdims=True)
    scale = lax.rsqrt(jnp.mean(centred * centred, axis=-1, keepdims=True) + norm_eps)
    return centred * scale, scale


def norm_back(upstream, unit, scale, gain):
    scaled = upstream * gain
    return scale * (
        scaled
        - jnp.mean(scaled, axis=-1, keepdims=True)
        - unit * jnp.mean(scaled * unit, axis=-1, keepdims=True)
    )


STRIP = 128


def strips(tokens, body):
    def step(j, carry):
        body(pl.ds(pl.multiple_of(j * STRIP, STRIP), STRIP))
        return carry

    lax.fori_loop(0, tokens // STRIP, step, 0)


def norm_kernel(hidden_ref, gain_ref, shift_ref, down_ref, low_ref, next_ref):
    def body(at):
        unit, _ = unit_of(hidden_ref[at, :])
        normed = unit * gain_ref[0:1, :] + shift_ref[0:1, :]
        low_ref[at, :] = normed.astype(bfloat)
        next_ref[at, :] = normed + down_ref[...]

    strips(hidden_ref.shape[0], body)


def feed_kernel(normed_ref, into_ref, bias_ref, down_ref, start_ref, act_ref, slope_ref, hidden_ref):
    hidden_units = into_ref.shape[1]
    tile = 256

    def step(j, carry):
        at = pl.ds(pl.multiple_of(j * tile, tile), tile)
        for k in range(2):
            strip = pl.ds(k * 256, 256)
            pre = dot(normed_ref[strip, :], into_ref[:, at]) + bias_ref[:, at]
            bell = jnp.exp(-0.5 * pre * pre)
            reach = 1.0 / (1.0 + 0.23164189 * jnp.abs(pre))
            tail = reach * (
                0.127414796
                + reach * (-0.142248368 + reach * (0.7107068705 + reach * (-0.7265760135 + reach * 0.5307027145)))
            )
            tail = tail * bell
            chance = jnp.where(pre >= 0, 1.0 - tail, tail)
            act_ref[strip, at] = (pre * chance).astype(bfloat)
            slope_ref[strip, at] = (chance + pre * bell * 0.3989422804014327).astype(bfloat)
        return carry

    lax.fori_loop(0, hidden_units // tile, step, 0)
    hidden_ref[...] = start_ref[...] + dot(act_ref[...], down_ref[...])


def feed(normed, into, bias, down, start):
    tokens, width = normed.shape
    units = into.shape[1]
    return call(
        feed_kernel,
        [shaped((tokens, units), bfloat), shaped((tokens, units), bfloat), shaped((tokens, width), single)],
        normed,
        into,
        bias,
        down,
        start,
    )


def add_columns(ref, row, value):
    ref[row : row + 1, :] += jnp.sum(value, axis=0, keepdims=True)


def turn_kernel(hidden_ref, gain_ref, shift_ref, upstream_ref, unit_ref, result_ref, grad_ref, branch_ref, sums_ref):
    sums_ref[...] = jnp.zeros_like(sums_ref)

    def body(at):
        unit, scale = unit_of(hidden_ref[at, :])
        gain = gain_ref[1:2, :]
        upstream = upstream_ref[at, :].astype(single)
        unit_ref[at, :] = unit
        result_ref[at, :] = (unit * gain + shift_ref[1:2, :]).astype(bfloat)
        grad = norm_back(upstream, unit, scale, gain)
        grad_ref[at, :] = grad
        branch_ref[at, :] = grad.astype(bfloat)
        add_columns(sums_ref, 0, upstream * unit)
        add_columns(sums_ref, 1, upstream)
        add_columns(sums_ref, 2, grad)

    strips(hidden_ref.shape[0], body)


def feed_back_kernel(branch_ref, down_ref, slope_ref, into_ref, start_ref, grad_ref, sums_ref, normed_ref):
    hidden_units = into_ref.shape[1]
    tile = 256

    def step(j, carry):
        at = pl.ds(pl.multiple_of(j * tile, tile), tile)
        pre = dot_cols(branch_ref[...], down_ref[at, :]) * slope_ref[:, at].astype(single)
        low = pre.astype(bfloat)
        grad_ref[:, at] = low
        sums_ref[:, at] = jnp.sum(low.astype(single), axis=0, keepdims=True)
        return carry

    lax.fori_loop(0, hidden_units // tile, step, 0)
    normed_ref[...] = start_ref[...] + dot_cols(grad_ref[...], into_ref[...])


def feed_back(branch, down, slope, into, start):
    tokens, width = branch.shape
    units = into.shape[1]
    return call(
        feed_back_kernel,
        [shaped((tokens, units), bfloat), shaped((1, units), single), shaped((tokens, width), single)],
        branch,
        down,
        slope,
        into,
        start,
    )


def norm_back_kernel(hidden_ref, gain_ref, upstream_ref, grad_ref, low_ref, sums_ref):
    sums_ref[...] = jnp.zeros_like(sums_ref)

    def body(at):
        unit, scale = unit_of(hidden_ref[at, :])
        upstream = upstream_ref[at, :]
        grad = norm_back(upstream, unit, scale, gain_ref[0:1, :])
        grad_ref[at, :] = grad
        low_ref[at, :] = grad.astype(bfloat)
        add_columns(sums_ref, 0, upstream * unit)
        add_columns(sums_ref, 1, upstream)
        add_columns(sums_ref, 2, grad)

    strips(hidden_ref.shape[0], body)


def attend_back_kernel(upstream_ref, out_w_ref, parts_ref, chance_ref, qkv_ref, start_ref, grad_ref, sums_ref, rows_ref, turned_ref):
    tokens = upstream_ref.shape[0]
    local = out_w_ref.shape[0]
    tile = 256
    factor = HEAD_DIM**-0.5

    def pair_step(pair, carry):
        at = pl.multiple_of(pair * PAIR, PAIR)
        lanes = pl.ds(at, PAIR)
        queries = parts_ref[0, :, lanes]
        keys_turned = parts_ref[1, :, lanes].T
        values = parts_ref[2, :, lanes]
        grad_context = dot_cols(upstream_ref[...], out_w_ref[lanes, :]).astype(bfloat)
        context_turned = grad_context.T
        owner = lax.broadcasted_iota(jnp.int32, (PAIR, tile), 0) // HEAD_DIM
        first_lane = lax.broadcasted_iota(jnp.int32, (tokens, PAIR), 1) < HEAD_DIM
        grads_k, grads_v = [], []
        for h in range(2):
            key_rows = keys_turned[h * HEAD_DIM : (h + 1) * HEAD_DIM]
            grad_k = jnp.zeros((tokens, PAIR), single)
            grad_v = jnp.zeros((tokens, PAIR), single)
            for q in range(tokens // tile):
                cut = slice(q * tile, (q + 1) * tile)
                picked = context_turned[:, cut]
                picked = jnp.where(owner == h, picked, jnp.zeros_like(picked))
                chances_low = chance_ref[pair * 2 + h, :, cut]
                chances = chances_low.astype(single)
                grad_chances = dot(values, picked)
                inner = jnp.sum(chances * grad_chances, axis=0, keepdims=True)
                grad_scores = (chances * (grad_chances - inner)).astype(bfloat)
                grad_v = grad_v + dot(chances_low, grad_context[cut, :])
                grad_k = grad_k + dot(grad_scores, queries[cut, :])
                turned_ref[pl.ds(pl.multiple_of(at + h * HEAD_DIM, HEAD_DIM), HEAD_DIM), cut] = (dot(key_rows, grad_scores) * factor).astype(bfloat)
            grads_k.append(grad_k)
            grads_v.append(grad_v)
        grad_k = (jnp.where(first_lane, grads_k[0], grads_k[1]) * factor).astype(bfloat)
        grad_v = jnp.where(first_lane, grads_v[0], grads_v[1]).astype(bfloat)
        grad_ref[:, pl.ds(pl.multiple_of(local + at, PAIR), PAIR)] = grad_k
        grad_ref[:, pl.ds(pl.multiple_of(2 * local + at, PAIR), PAIR)] = grad_v
        return carry

    lax.fori_loop(0, local // PAIR, pair_step, 0)
    grad_ref[:, 0:local] = turned_ref[...].T
    sums_ref[...] = jnp.sum(grad_ref[...].astype(single), axis=0, keepdims=True)
    total = start_ref[...]
    for part in range(3):
        total = total + dot_cols(grad_ref[:, part * local : (part + 1) * local], qkv_ref[part])
    rows_ref[...] = total


def attend_back(upstream, out, parts, chances, qkv, start):
    tokens, width = upstream.shape
    local = out.shape[0]
    return call(
        attend_back_kernel,
        [shaped((tokens, 3 * local), bfloat), shaped((1, 3 * local), single), shaped((tokens, width), single)],
        upstream,
        out,
        parts,
        chances,
        qkv,
        start,
        scratch=[pltpu.VMEM((local, tokens), bfloat)],
    )


def body(
    inputs,
    lengths,
    w_qkv,
    b_qv,
    w_out,
    b_out,
    ln_gains,
    ln_biases,
    w_in,
    b_in,
    w_down,
    b_down,
    cotangent,
):
    size = lax.axis_size("dp")
    me = lax.axis_index("dp")
    side = lax.axis_index("tensor")
    tokens, width = inputs.shape[1:]
    local = w_qkv.shape[2]
    units = w_in.shape[1]
    rows = lax.dynamic_index_in_dim(inputs, side, 0, keepdims=False)
    length = lax.dynamic_slice_in_dim(lengths, side, 1)
    upstream = lax.dynamic_index_in_dim(cotangent, side, 0, keepdims=False)

    qkv_own = jnp.transpose(w_qkv, (1, 0, 2))
    small_other = swap_x(jnp.concatenate([b_qv.reshape(-1), b_in]))
    b_qv_other, b_in_other = small_other[: 2 * local].reshape(2, local), small_other[2 * local :]
    qkv_other = place([fetch_spread(qkv_own, me, size, (4, 2))], qkv_own.shape)
    out_other = place([fetch_direct(w_out, me, size)], w_out.shape)
    in_other = place([fetch_spread(w_in, me, size, (2, 4))], w_in.shape)
    cut, end = units // 2, 3 * units // 4
    down_other = place(
        [
            fetch_spread(w_down[:cut], me, size, (4, 2)),
            fetch_spread(w_down[cut:end], me, size, (2, 4), base=cut),
            fetch_direct(w_down[end:], me, size, base=end),
        ],
        w_down.shape,
    )
    sides = (
        (qkv_own, b_qv, w_out, w_in, b_in.reshape(1, -1), w_down),
        (qkv_other, b_qv_other, out_other, in_other, b_in_other.reshape(1, -1), down_other),
    )

    bits = size.bit_length() - 1
    share = width // size
    block_of = jnp.array([reverse_bits(p, bits) for p in range(size)], jnp.int32) ^ me
    source = (block_of[:, None] * share + jnp.arange(share)[None, :]).reshape(-1, 1)

    heads = []
    hidden_one = rows.astype(single) + b_out
    for qkv, bias, out, _, _, _ in sides:
        parts, chances, context, hidden_one = attend(length, rows, qkv, bias, out, hidden_one)
        heads.append((parts, chances, context))
    normed_low, hidden_two = call(
        norm_kernel,
        [shaped((tokens, width), bfloat), shaped((tokens, width), single)],
        hidden_one,
        ln_gains,
        ln_biases,
        b_down.reshape(1, -1),
    )
    acts = []
    for _, _, _, into, bias, down in sides:
        act, slope, hidden_two = feed(normed_low, into, bias, down, hidden_two)
        acts.append((act, slope))
    unit_two, result, grad_two, branch, sums_two = call(
        turn_kernel,
        [
            shaped((tokens, width), single),
            shaped((tokens, width), bfloat),
            shaped((tokens, width), single),
            shaped((tokens, width), bfloat),
            shaped((3, width), single),
        ],
        hidden_two,
        ln_gains,
        ln_biases,
        upstream,
    )
    result_other = (swap_x(unit_two) * ln_gains[1] + ln_biases[1]).astype(bfloat)

    share_down = scatter_x_first(relative(branch, source), acts[0][0], acts[1][0], size)
    grad_pres, unit_sums = [], []
    grad_normed = grad_two
    for (_, slope), (_, _, _, into, _, down) in zip(acts, sides):
        grad_pre, unit_sum, grad_normed = feed_back(branch, down, slope, into, grad_normed)
        grad_pres.append(grad_pre)
        unit_sums.append(unit_sum)
    share_in = scatter_y_first(relative(normed_low, source), grad_pres[0], grad_pres[1], size)
    grad_one, attended, sums_one = call(
        norm_back_kernel,
        [shaped((tokens, width), single), shaped((tokens, width), bfloat), shaped((3, width), single)],
        hidden_one,
        ln_gains,
        grad_normed,
    )
    share_out = scatter_x_first(relative(attended, source), heads[0][2], heads[1][2], size)
    grad_rows = grad_one
    grad_projs, proj_sums = [], []
    for (parts, chances, _), (qkv, _, out, _, _, _) in zip(heads, sides):
        grad_proj, proj_sum, grad_rows = attend_back(attended, out, parts, chances, qkv, grad_rows)
        grad_projs.append(grad_proj)
        proj_sums.append(proj_sum)
    grad_rows_other = swap_x(grad_rows)
    share_qkv = scatter_y_first(relative(rows, source), grad_projs[0], grad_projs[1], size)

    every = jnp.concatenate([sums_one.reshape(-1), sums_two.reshape(-1)])
    vectors = jnp.concatenate([every, unit_sums[0].reshape(-1)])
    vectors_other = swap_x(jnp.concatenate([every, unit_sums[1].reshape(-1)]))
    vectors = sum_all(vectors + vectors_other, size)
    qv_own, qv_other = (
        jnp.concatenate([part[0, :local], part[0, 2 * local :]]) for part in proj_sums
    )
    grad_b_qv = sum_all(qv_own + swap_x(qv_other), size).reshape(2, local)
    gain_one, shift_one, b_out_g, gain_two, shift_two, b_down_g = (
        vectors[k * width : (k + 1) * width] for k in range(6)
    )

    def both(mine, other):
        mine, other = mine[None], other[None]
        return jnp.where(
            side == 0,
            jnp.concatenate([mine, other], axis=0),
            jnp.concatenate([other, mine], axis=0),
        )

    return (
        both(result, result_other),
        both(grad_rows, grad_rows_other),
        share_qkv.reshape(-1, 3, local),
        grad_b_qv,
        share_out.T,
        b_out_g,
        jnp.stack([gain_one, gain_two]),
        jnp.stack([shift_one, shift_two]),
        share_in,
        vectors[6 * width :],
        share_down.T,
        b_down_g,
    )


def solution(mesh):
    placed = (
        P("dp", None, None),
        P("dp"),
        P(None, None, "tensor"),
        P(None, "tensor"),
        P("tensor", None),
        P(),
        P(),
        P(),
        P(None, "tensor"),
        P("tensor"),
        P("tensor", None),
        P(),
        P("dp", None, None),
    )
    return jax.shard_map(
        body,
        mesh=mesh,
        in_specs=placed,
        out_specs=(
            P("dp", None, None),
            P("dp", None, None),
            P("dp", None, "tensor"),
            P(None, "tensor"),
            P("tensor", "dp"),
            P(),
            P(),
            P(),
            P("dp", "tensor"),
            P("tensor"),
            P("tensor", "dp"),
            P(),
        ),
        check_vma=False,
    )
```

time: 596 us -> 551 us (0.924); the launches traced: 587 us -> 549 us
  Pallas kernels: 37.2 us -> 139 us
  matrix products: 98.5 us -> 0 us
  waiting for transfers between devices: 314 us -> 270 us
  other arithmetic: 43.8 us -> 30.1 us
  starting transfers between devices: 52.1 us -> 62.6 us
  local copies, waits for them, and re-layouts: 39 us -> 45.7 us
    pallas_call x5 -> x31, Pallas kernels: 37.2 us -> 139 us  [call(): pl.pallas_call(kernel, out_shape=outs, grid=grid, in_specs=[pl.BlockSpec(...]
    dot_general x48 -> x0, matrix products: 98.5 us -> none  [the longest x16 28 us: dot_rows(): lax.dot_general(left, right, (((0,), (0,)), ((), ())), preferred_element_...]
    ppermute x14 -> x15, waiting for transfers between devices: 139 us -> 77 us  [swap_x(): return lax.ppermute(value, 'tensor', [(0, 1), (1, 0)])]
    ppermute x48 -> x44, waiting for transfers between devices: 175 us -> 193 us  [swap_dp(): return lax.ppermute(value, 'dp', [(i, i ^ mask) for i in range(size)])]
    unnamed x240 -> x172, local copies, waits for them, and re-layouts: 21.6 us -> 32.6 us
    reduce_sum x8 -> x0, other arithmetic: 8.69 us -> none  [the longest x4 6.36 us: columns(): return jnp.sum(value.astype(single), axis=0)]
    concatenate x5 -> x0, local copies, waits for them, and re-layouts: 8.4 us -> none  [the longest x3 8.39 us: fetch_spread(): held = jnp.concatenate([held, swap_dp(held, 1, size)], axis=0)]
    convert_element_type x8 -> x4, other arithmetic: 9.28 us -> 2.93 us  [fetch_spread(): lax.dynamic_slice_in_dim(own, rank * rows, rows, axis=own.ndim - 2)]
  transfers between devices with their start and end apart: 62 -> 59, of which waited for: 26 -> 23; matrix products, arithmetic and copies ran while one was open for 17% -> 7% of each run, Pallas kernels for 5% -> 19%
where the time goes in v2:
time: 551 us; the launch traced here: 549 us
  waiting for transfers between devices  270 us (49%)
  Pallas kernels  139 us (25%)
  starting transfers between devices  62.6 us (11%)
  local copies, waits for them, and re-layouts  45.7 us (8%)
  other arithmetic  30.1 us (5%)
    ppermute x44, waiting for transfers between devices, swap_dp(): return lax.ppermute(value, 'dp', [(i, i ^ mask) for i in range(size)])  193 us
    pallas_call x31, Pallas kernels, call(): pl.pallas_call(kernel, out_shape=outs, grid=grid, in_specs=[pl.BlockSpec(...  139 us
    ppermute x15, waiting for transfers between devices, swap_x(): return lax.ppermute(value, 'tensor', [(0, 1), (1, 0)])  77 us
    ppermute x44, starting transfers between devices, swap_dp(): return lax.ppermute(value, 'dp', [(i, i ^ mask) for i in range(size)])  41.6 us
    unnamed x172, local copies, waits for them, and re-layouts  32.6 us
    ppermute x15, starting transfers between devices, swap_x(): return lax.ppermute(value, 'tensor', [(0, 1), (1, 0)])  21 us
  transfers between devices with their start and end apart: 59, of which 23 were waited for; matrix products, arithmetic and copies ran while one was open for 7% of the time, Pallas kernels for 19%

profile of v2, /device:TPU:0, one launch (start us, length us, event | category | flops | bytes accessed | tf_op | source)
XLA Modules:
  0.0 549.1 jit_solution(12851252163231848993)
XLA Ops:
  9.5 9.6 %collective-permute-done.8 = f32[96,1536]{1,0:T(8,128)} collective-permute-done((f32[96,1536]{1,0:T(8,128)S(1)}, f32[96,1536]{1,0:T(8,128)}, u32[]{:S(2)}, u32[]{:S(2)}) %collective-permute-start.8) | collective-permute-done | bytes 589856 | tf_op jit(solution)/shard_map/ppermute | solution.py:54
  32.4 12.1 %collective-permute-done.18 = f32[48,768]{1,0:T(8,128)S(1)} collective-permute-done((f32[48,768]{1,0:T(8,128)S(1)}, f32[48,768]{1,0:T(8,128)S(1)}, u32[]{:S(2)}, u32[]{:S(2)}) %collective-permute-start.18) | collective-permute-done | bytes 147488 | tf_op jit(solution)/shard_map/ppermute | solution.py:54
  57.2 29.2 %collective-permute-done.14 = f32[1,96,768]{2,1,0:T(8,128)S(1)} collective-permute-done((f32[1,96,768]{2,1,0:T(8,128)S(1)}, f32[1,96,768]{2,1,0:T(8,128)S(1)}, u32[]{:S(2)}, u32[]{:S(2)}) %collective-permute-start.14) | collective-permute-done | bytes 294944 | tf_op jit(solution)/shard_map/ppermute | solution.py:50
  95.2 29.8 %collective-permute-done.15.refs_1_ = f32[2,96,768]{2,1,0:T(8,128)S(1)} collective-permute-done((f32[2,96,768]{2,1,0:T(8,128)S(1)}, f32[2,96,768]{2,1,0:T(8,128)S(1)}, u32[]{:S(2)}, u32[]{:S(2)}) %collective-permute-start.15) | collective-permute-done | bytes 589856 | tf_op jit(solution)/shard_map/ppermute | solution.py:50
  128.0 11.5 %shard_map.231 = (bf16[3,512,384]{2,1,0:T(8,128)(2,1)S(1)}, bf16[6,512,512]{2,1,0:T(8,128)(2,1)}, bf16[512,384]{1,0:T(8,128)(2,1)S(1)}, f32[512,768]{1,0:T(8,128)S(1)}) custom-call(s32[1]{0:T(128)} %dynamic_slice.28.length_ref, bf16[512,768]{1,0:T(8,128)(2,1)S(1)} %get-tuple-element.129.rows_ref.value_ref, bf16[3,768,384]{2,1,0:T(8,128)(2,1)} %bitcast.60, ...), custom_call_target="tpu_custom_call" | custom-call | flops 1000 | bytes 1000 | tf_op jit(solution)/shard_map/pallas_call | solution.py:37
  159.6 11.4 %shard_map.232 = (bf16[3,512,384]{2,1,0:T(8,128)(2,1)S(1)}, bf16[6,512,512]{2,1,0:T(8,128)(2,1)}, bf16[512,384]{1,0:T(8,128)(2,1)S(1)}, f32[512,768]{1,0:T(8,128)S(1)}) custom-call(s32[1]{0:T(128)} %dynamic_slice.28.length_ref, bf16[512,768]{1,0:T(8,128)(2,1)S(1)} %get-tuple-element.129.rows_ref.value_ref, bf16[3,768,384]{2,1,0:T(8,128)(2,1)} %copy-done.2, ...), custom_call_target="tpu_custom_call" | custom-call | flops 1000 | bytes 1000 | tf_op jit(solution)/shard_map/pallas_call | solution.py:37
  174.9 8.8 %shard_map.236 = (bf16[512,1536]{1,0:T(8,128)(2,1)S(1)}, bf16[512,1536]{1,0:T(8,128)(2,1)S(1)}, f32[512,768]{1,0:T(8,128)S(1)}) custom-call(bf16[512,768]{1,0:T(8,128)(2,1)S(1)} %get-tuple-element.58.normed_ref.value_ref, bf16[768,1536]{1,0:T(8,128)(2,1)} %into_ref.3, f32[1,1536]{1,0:T(1,128)S(1)} %copy-done.62, bf16[1536,768]{1,0:T(8,128)(2,1)} %down_ref.3, ...), custom_call_target="tpu_custom_call" | custom-call | flops 1000 | bytes 1000 | tf_op jit(solution)/shard_map/pallas_call | solution.py:37
  189.5 8.8 %shard_map.237 = (bf16[512,1536]{1,0:T(8,128)(2,1)S(1)}, bf16[512,1536]{1,0:T(8,128)(2,1)S(1)}, f32[512,768]{1,0:T(8,128)S(1)}) custom-call(bf16[512,768]{1,0:T(8,128)(2,1)S(1)} %get-tuple-element.58.normed_ref.value_ref, bf16[768,1536]{1,0:T(8,128)(2,1)} %shard_map.234.into_ref, f32[1,1536]{1,0:T(1,128)S(1)} %reshape.91.bias_ref, ...), custom_call_target="tpu_custom_call" | custom-call | flops 1000 | bytes 1000 | tf_op jit(solution)/shard_map/pallas_call | solution.py:37
  200.7 4.6 shard_map.238
  207.1 6.7 %shard_map.239 = (bf16[512,1536]{1,0:T(8,128)(2,1)S(1)}, f32[1,1536]{1,0:T(1,128)S(1)}, f32[512,768]{1,0:T(8,128)S(1)}) custom-call(bf16[512,768]{1,0:T(8,128)(2,1)S(1)} %get-tuple-element.64.branch_ref.value_ref, bf16[1536,768]{1,0:T(8,128)(2,1)} %down_ref.3, bf16[512,1536]{1,0:T(8,128)(2,1)S(1)} %get-tuple-element.66.slope_ref, ...), custom_call_target="tpu_custom_call" | custom-call | flops 1000 | bytes 1000 | tf_op jit(solution)/shard_map/pallas_call | solution.py:37
  217.5 6.7 %shard_map.240 = (bf16[512,1536]{1,0:T(8,128)(2,1)S(1)}, f32[1,1536]{1,0:T(1,128)S(1)}, f32[512,768]{1,0:T(8,128)S(1)}) custom-call(bf16[512,768]{1,0:T(8,128)(2,1)S(1)} %get-tuple-element.64.branch_ref.value_ref, bf16[1536,768]{1,0:T(8,128)(2,1)} %shard_map.235.down_ref, bf16[512,1536]{1,0:T(8,128)(2,1)S(1)} %copy-done.37, ...), custom_call_target="tpu_custom_call" | custom-call | flops 1000 | bytes 1000 | tf_op jit(solution)/shard_map/pallas_call | solution.py:37
  234.2 12.2 %shard_map.242 = (bf16[512,1152]{1,0:T(8,128)(2,1)S(1)}, f32[1,1152]{1,0:T(1,128)S(1)}, f32[512,768]{1,0:T(8,128)S(1)}) custom-call(bf16[512,768]{1,0:T(8,128)(2,1)S(1)} %get-tuple-element.70.upstream_ref.value_ref, bf16[384,768]{1,0:T(8,128)(2,1)S(1)} %copy-done.16, bf16[3,512,384]{2,1,0:T(8,128)(2,1)S(1)} %copy-done.45, ...), custom_call_target="tpu_custom_call" | custom-call | flops 1000 | bytes 1000 | tf_op jit(solution)/shard_map/pallas_call | solution.py:37
  248.2 13.7 %shard_map.243 = (bf16[512,1152]{1,0:T(8,128)(2,1)S(1)}, f32[1,1152]{1,0:T(1,128)S(1)}, f32[512,768]{1,0:T(8,128)}) custom-call(bf16[512,768]{1,0:T(8,128)(2,1)S(1)} %get-tuple-element.70.upstream_ref.value_ref, bf16[384,768]{1,0:T(8,128)(2,1)S(1)} %shard_map.230.out_w_ref, bf16[3,512,384]{2,1,0:T(8,128)(2,1)S(1)} %copy-done.47, ...), custom_call_target="tpu_custom_call" | custom-call | flops 1000 | bytes 1000 | tf_op jit(solution)/shard_map/pallas_call | solution.py:37
  320.8 6.4 %shard_map.246 = (f32[2,192,1152]{2,1,0:T(8,128)S(1)}, f32[2,192,1152]{2,1,0:T(8,128)}) custom-call(bf16[768,512]{1,0:T(8,128)(2,1)S(1)} %shard_map.244.refs_0_, bf16[512,1152]{1,0:T(8,128)(2,1)S(1)} %copy-done.12, bf16[512,1152]{1,0:T(8,128)(2,1)S(1)} %copy-done.14, f32[2,384,1152]{2,1,0:T(8,128)} %collective-permute-done.27.refs_3_), custom_call_target="tpu_custom_call" | custom-call | flops 1000 | bytes 1000 | tf_op jit(solution)/shard_map/pallas_call | solution.py:37
  328.7 41.0 %collective-permute-done.39.refs_3_ = f32[384,384]{1,0:T(8,128)S(1)} collective-permute-done((f32[384,384]{1,0:T(8,128)S(1)}, f32[384,384]{1,0:T(8,128)S(1)}, u32[]{:S(2)}, u32[]{:S(2)}) %collective-permute-start.39) | collective-permute-done | bytes 589856 | tf_op jit(solution)/shard_map/ppermute | solution.py:54
  371.7 6.5 %shard_map.254 = (f32[2,192,1536]{2,1,0:T(8,128)S(1)}, f32[2,192,1536]{2,1,0:T(8,128)}) custom-call(bf16[768,512]{1,0:T(8,128)(2,1)S(1)} %shard_map.252.refs_0_, bf16[512,1536]{1,0:T(8,128)(2,1)S(1)} %copy-done.8, bf16[512,1536]{1,0:T(8,128)(2,1)S(1)} %copy-done.10, f32[2,384,1536]{2,1,0:T(8,128)} %collective-permute-done.48.refs_3_), custom_call_target="tpu_custom_call" | custom-call | flops 1000 | bytes 1000 | tf_op jit(solution)/shard_map/pallas_call | solution.py:37
  388.8 47.4 %collective-permute-done.40 = f32[192,384]{1,0:T(8,128)S(1)} collective-permute-done((f32[192,384]{1,0:T(8,128)S(1)}, f32[192,384]{1,0:T(8,128)S(1)}, u32[]{:S(2)}, u32[]{:S(2)}) %collective-permute-start.40) | collective-permute-done | bytes 294944 | tf_op jit(solution)/shard_map/ppermute | solution.py:50
  444.5 5.2 maximum_select_fusion
  453.7 4.9 collective-permute-done.56
  466.9 19.9 %collective-permute-done.57 = f32[96,1536]{1,0:T(8,128)S(1)} collective-permute-done((f32[96,1536]{1,0:T(8,128)S(1)}, f32[96,1536]{1,0:T(8,128)S(1)}, u32[]{:S(2)}, u32[]{:S(2)}) %collective-permute-start.57) | collective-permute-done | bytes 589856 | tf_op jit(solution)/shard_map/ppermute | solution.py:50
  487.8 19.0 %collective-permute-done.30 = f32[2,48,1152]{2,1,0:T(8,128)S(1)} collective-permute-done((f32[2,48,1152]{2,1,0:T(8,128)S(1)}, f32[2,48,1152]{2,1,0:T(8,128)S(1)}, u32[]{:S(2)}, u32[]{:S(2)}) %collective-permute-start.30) | collective-permute-done | bytes 442400 | tf_op jit(solution)/shard_map/ppermute | solution.py:50
  506.8 5.1 collective-permute-done.50
  515.1 24.1 %collective-permute-done.51 = f32[2,48,1536]{2,1,0:T(8,128)S(1)} collective-permute-done((f32[2,48,1536]{2,1,0:T(8,128)S(1)}, f32[2,48,1536]{2,1,0:T(8,128)S(1)}, u32[]{:S(2)}, u32[]{:S(2)}) %collective-permute-start.51) | collective-permute-done | bytes 589856 | tf_op jit(solution)/shard_map/ppermute | solution.py:50
  541.6 6.7 %collective-permute-done.52 = f32[48,1536]{1,0:T(8,128)S(1)} collective-permute-done((f32[48,1536]{1,0:T(8,128)S(1)}, f32[48,1536]{1,0:T(8,128)S(1)}, u32[]{:S(2)}, u32[]{:S(2)}) %collective-permute-start.52) | collective-permute-done | bytes 294944 | tf_op jit(solution)/shard_map/ppermute | solution.py:54
  (384 shorter events, 195.9 us)
Async XLA Ops:
  9.4 44.0 %collective-permute-start.6 = (f32[192,768]{1,0:T(8,128)S(1)}, f32[192,768]{1,0:T(8,128)}, u32[]{:S(2)}, u32[]{:S(2)}) collective-permute-start(f32[192,768]{1,0:T(8,128)S(1)} %dynamic-slice_convert_fusion.2), channel_id=1, source_target_pairs={{0,1},{1,0},{2,3},{3,2},{4,5},{5,4},{6,7},{7,6},{8,9},{9,8},{10,11... | collective-permute-start | bytes 1769480 | tf_op jit(solution)/shard_map/ppermute | solution.py:54
  44.6 47.1 %collective-permute-start.23 = (f32[192,768]{1,0:T(8,128)S(1)}, f32[192,768]{1,0:T(8,128)}, u32[]{:S(2)}, u32[]{:S(2)}) collective-permute-start(f32[192,768]{1,0:T(8,128)S(1)} %dynamic-slice_convert_fusion), channel_id=1, source_target_pairs={{0,1},{1,0},{2,3},{3,2},{4,5},{5,4},{6,7},{7,6},{8,9},{9,8},{10,11... | collective-permute-start | bytes 1769480 | tf_op jit(solution)/shard_map/ppermute | solution.py:54
  50.9 74.1 %collective-permute-start.10 = (f32[2,96,1536]{2,1,0:T(8,128)}, f32[2,96,1536]{2,1,0:T(8,128)}, u32[]{:S(2)}, u32[]{:S(2)}) collective-permute-start(f32[2,96,1536]{2,1,0:T(8,128)} %pad_maximum_fusion.refs_0_), channel_id=1, source_target_pairs={{0,8},{2,10},{4,12},{6,14},{8,0},{10,2},{12,4},{14,6},{16,24},{18,... | collective-permute-start | bytes 3538952 | tf_op jit(solution)/shard_map/ppermute | solution.py:50
  53.0 33.4 %collective-permute-start.14 = (f32[1,96,768]{2,1,0:T(8,128)S(1)}, f32[1,96,768]{2,1,0:T(8,128)S(1)}, u32[]{:S(2)}, u32[]{:S(2)}) collective-permute-start(f32[1,96,768]{2,1,0:T(8,128)S(1)} %bitcast.63), channel_id=1, source_target_pairs={{0,8},{2,10},{4,12},{6,14},{8,0},{10,2},{12,4},{14,6},{16,24},{18,... | collective-permute-start | bytes 884744 | tf_op jit(solution)/shard_map/ppermute | solution.py:50
  53.4 36.6 %collective-permute-start.20 = (f32[2,48,768]{2,1,0:T(8,128)S(1)}, f32[2,48,768]{2,1,0:T(8,128)S(1)}, u32[]{:S(2)}, u32[]{:S(2)}) collective-permute-start(f32[2,48,768]{2,1,0:T(8,128)S(1)} %pad_maximum_fusion.3.refs_4_), channel_id=1, source_target_pairs={{0,8},{2,10},{4,12},{6,14},{8,0},{10,2},{12,4},{14,6},{16,24},{18,... | collective-permute-start | bytes 884744 | tf_op jit(solution)/shard_map/ppermute | solution.py:50
  55.2 34.9 %collective-permute-start.21 = (f32[2,48,768]{2,1,0:T(8,128)S(1)}, f32[2,48,768]{2,1,0:T(8,128)S(1)}, u32[]{:S(2)}, u32[]{:S(2)}) collective-permute-start(f32[2,48,768]{2,1,0:T(8,128)S(1)} %pad_maximum_fusion.3.refs_4_), channel_id=1, source_target_pairs={{0,2},{2,0},{4,6},{6,4},{8,10},{10,8},{12,14},{14,12},{16,18},{18,... | collective-permute-start | bytes 884744 | tf_op jit(solution)/shard_map/ppermute | solution.py:50
  90.1 36.1 %collective-permute-start.2 = (f32[2,3,96,384]{3,2,1,0:T(8,128)}, f32[2,3,96,384]{3,2,1,0:T(8,128)}, u32[]{:S(2)}, u32[]{:S(2)}) collective-permute-start(f32[2,3,96,384]{3,2,1,0:T(8,128)} %pad_maximum_fusion.1.refs_0_), channel_id=1, source_target_pairs={{0,4},{2,6},{4,0},{6,2},{8,12},{10,14},{12,8},{14,10},{16,20},{18,... | collective-permute-start | bytes 2654216 | tf_op jit(solution)/shard_map/ppermute | solution.py:50
  91.6 33.3 %collective-permute-start.15 = (f32[2,96,768]{2,1,0:T(8,128)S(1)}, f32[2,96,768]{2,1,0:T(8,128)S(1)}, u32[]{:S(2)}, u32[]{:S(2)}) collective-permute-start(f32[2,96,768]{2,1,0:T(8,128)S(1)} %pad_maximum_fusion.2.refs_0_), channel_id=1, source_target_pairs={{0,4},{2,6},{4,0},{6,2},{8,12},{10,14},{12,8},{14,10},{16,20},{18,... | collective-permute-start | bytes 1769480 | tf_op jit(solution)/shard_map/ppermute | solution.py:50
  93.0 33.2 %collective-permute-start.16 = (f32[2,96,768]{2,1,0:T(8,128)S(1)}, f32[2,96,768]{2,1,0:T(8,128)}, u32[]{:S(2)}, u32[]{:S(2)}) collective-permute-start(f32[2,96,768]{2,1,0:T(8,128)S(1)} %pad_maximum_fusion.2.refs_0_), channel_id=1, source_target_pairs={{0,2},{2,0},{4,6},{6,4},{8,10},{10,8},{12,14},{14,12},{16,18},{18,... | collective-permute-start | bytes 1769480 | tf_op jit(solution)/shard_map/ppermute | solution.py:50
  94.7 49.6 %collective-permute-start.24 = (f32[1,192,768]{2,1,0:T(8,128)}, f32[1,192,768]{2,1,0:T(8,128)}, u32[]{:S(2)}, u32[]{:S(2)}) collective-permute-start(f32[1,192,768]{2,1,0:T(8,128)} %bitcast.28.refs_8_), channel_id=1, source_target_pairs={{0,2},{2,0},{4,6},{6,4},{8,10},{10,8},{12,14},{14,12},{16,18},{18,... | collective-permute-start | bytes 1769480 | tf_op jit(solution)/shard_map/ppermute | solution.py:50
  125.0 59.9 %collective-permute-start.11 = (f32[2,96,1536]{2,1,0:T(8,128)}, f32[2,96,1536]{2,1,0:T(8,128)}, u32[]{:S(2)}, u32[]{:S(2)}) collective-permute-start(f32[2,96,1536]{2,1,0:T(8,128)} %pad_maximum_fusion.refs_0_), channel_id=1, source_target_pairs={{0,2},{2,0},{4,6},{6,4},{8,10},{10,8},{12,14},{14,12},{16,18},{18,... | collective-permute-start | bytes 3538952 | tf_op jit(solution)/shard_map/ppermute | solution.py:50
  125.0 59.8 %collective-permute-start.12 = (f32[2,96,1536]{2,1,0:T(8,128)}, f32[2,96,1536]{2,1,0:T(8,128)}, u32[]{:S(2)}, u32[]{:S(2)}) collective-permute-start(f32[2,96,1536]{2,1,0:T(8,128)} %collective-permute-done.10.refs_1_), channel_id=1, source_target_pairs={{0,2},{2,0},{4,6},{6,4},{8,10},{10,8},{12,14},{14,12},{16,18},{18,... | collective-permute-start | bytes 3538952 | tf_op jit(solution)/shard_map/ppermute | solution.py:50
  228.9 142.2 %collective-permute-start.48 = (f32[2,384,1536]{2,1,0:T(8,128)}, f32[2,384,1536]{2,1,0:T(8,128)}, u32[]{:S(2)}, u32[]{:S(2)}) collective-permute-start(f32[2,384,1536]{2,1,0:T(8,128)} %shard_map.253), channel_id=1, source_target_pairs={{0,2},{2,0},{4,6},{6,4},{8,10},{10,8},{12,14},{14,12},{16,18},{18,... | collective-permute-start | bytes 14155784 | tf_op jit(solution)/shard_map/ppermute | solution.py:50
  266.3 53.9 %collective-permute-start.27 = (f32[2,384,1152]{2,1,0:T(8,128)}, f32[2,384,1152]{2,1,0:T(8,128)}, u32[]{:S(2)}, u32[]{:S(2)}) collective-permute-start(f32[2,384,1152]{2,1,0:T(8,128)} %shard_map.245), channel_id=1, source_target_pairs={{0,2},{2,0},{4,6},{6,4},{8,10},{10,8},{12,14},{14,12},{16,18},{18,... | collective-permute-start | bytes 10616840 | tf_op jit(solution)/shard_map/ppermute | solution.py:50
  276.7 101.6 %collective-permute-start.53 = (f32[384,1536]{1,0:T(8,128)}, f32[384,1536]{1,0:T(8,128)}, u32[]{:S(2)}, u32[]{:S(2)}) collective-permute-start(f32[384,1536]{1,0:T(8,128)} %copy-done.23), channel_id=1, source_target_pairs={{0,2},{2,0},{4,6},{6,4},{8,10},{10,8},{12,14},{14,12},{16,18},{18,... | collective-permute-start | bytes 7077896 | tf_op jit(solution)/shard_map/ppermute | solution.py:50
  305.9 74.4 %collective-permute-start.55 = (f32[384,1536]{1,0:T(8,128)S(1)}, f32[384,1536]{1,0:T(8,128)S(1)}, u32[]{:S(2)}, u32[]{:S(2)}) collective-permute-start(f32[384,1536]{1,0:T(8,128)S(1)} %shard_map.258), channel_id=1, source_target_pairs={{0,1},{1,0},{2,3},{3,2},{4,5},{5,4},{6,7},{7,6},{8,9},{9,8},{10,11... | collective-permute-start | bytes 7077896 | tf_op jit(solution)/shard_map/ppermute | solution.py:54
  320.2 49.5 %collective-permute-start.39 = (f32[384,384]{1,0:T(8,128)S(1)}, f32[384,384]{1,0:T(8,128)S(1)}, u32[]{:S(2)}, u32[]{:S(2)}) collective-permute-start(f32[384,384]{1,0:T(8,128)S(1)} %shard_map.250), channel_id=1, source_target_pairs={{0,1},{1,0},{2,3},{3,2},{4,5},{5,4},{6,7},{7,6},{8,9},{9,8},{10,11... | collective-permute-start | bytes 1769480 | tf_op jit(solution)/shard_map/ppermute | solution.py:54
  327.2 111.8 %collective-permute-start.28 = (f32[2,192,1152]{2,1,0:T(8,128)}, f32[2,192,1152]{2,1,0:T(8,128)}, u32[]{:S(2)}, u32[]{:S(2)}) collective-permute-start(f32[2,192,1152]{2,1,0:T(8,128)} %get-tuple-element.81), channel_id=1, source_target_pairs={{0,4},{2,6},{4,0},{6,2},{8,12},{10,14},{12,8},{14,10},{16,20},{18,... | collective-permute-start | bytes 5308424 | tf_op jit(solution)/shard_map/ppermute | solution.py:50
  369.7 72.7 %collective-permute-start.25 = (f32[512,768]{1,0:T(8,128)}, f32[512,768]{1,0:T(8,128)}, u32[]{:S(2)}, u32[]{:S(2)}) collective-permute-start(f32[512,768]{1,0:T(8,128)} %get-tuple-element.63), channel_id=1, source_target_pairs={{0,1},{1,0},{2,3},{3,2},{4,5},{5,4},{6,7},{7,6},{8,9},{9,8},{10,11... | collective-permute-start | bytes 4718600 | tf_op jit(solution)/shard_map/ppermute | solution.py:54
  371.1 73.3 %collective-permute-start.26 = (f32[512,768]{1,0:T(8,128)}, f32[512,768]{1,0:T(8,128)}, u32[]{:S(2)}, u32[]{:S(2)}) collective-permute-start(f32[512,768]{1,0:T(8,128)} %get-tuple-element.77), channel_id=1, source_target_pairs={{0,1},{1,0},{2,3},{3,2},{4,5},{5,4},{6,7},{7,6},{8,9},{9,8},{10,11... | collective-permute-start | bytes 4718600 | tf_op jit(solution)/shard_map/ppermute | solution.py:54
  378.3 82.7 %collective-permute-start.49 = (f32[2,192,1536]{2,1,0:T(8,128)}, f32[2,192,1536]{2,1,0:T(8,128)}, u32[]{:S(2)}, u32[]{:S(2)}) collective-permute-start(f32[2,192,1536]{2,1,0:T(8,128)} %get-tuple-element.95), channel_id=1, source_target_pairs={{0,4},{2,6},{4,0},{6,2},{8,12},{10,14},{12,8},{14,10},{16,20},{18,... | collective-permute-start | bytes 7077896 | tf_op jit(solution)/shard_map/ppermute | solution.py:50
  381.7 54.6 %collective-permute-start.40 = (f32[192,384]{1,0:T(8,128)S(1)}, f32[192,384]{1,0:T(8,128)S(1)}, u32[]{:S(2)}, u32[]{:S(2)}) collective-permute-start(f32[192,384]{1,0:T(8,128)S(1)} %get-tuple-element.87), channel_id=1, source_target_pairs={{0,4},{2,6},{4,0},{6,2},{8,12},{10,14},{12,8},{14,10},{16,20},{18,... | collective-permute-start | bytes 884744 | tf_op jit(solution)/shard_map/ppermute | solution.py:50
  463.2 48.7 %collective-permute-start.50 = (f32[2,96,1536]{2,1,0:T(8,128)S(1)}, f32[2,96,1536]{2,1,0:T(8,128)S(1)}, u32[]{:S(2)}, u32[]{:S(2)}) collective-permute-start(f32[2,96,1536]{2,1,0:T(8,128)S(1)} %slice.181), channel_id=1, source_target_pairs={{0,8},{2,10},{4,12},{6,14},{8,0},{10,2},{12,4},{14,6},{16,24},{18,... | collective-permute-start | bytes 3538952 | tf_op jit(solution)/shard_map/ppermute | solution.py:50
  466.9 39.9 %collective-permute-start.30 = (f32[2,48,1152]{2,1,0:T(8,128)S(1)}, f32[2,48,1152]{2,1,0:T(8,128)S(1)}, u32[]{:S(2)}, u32[]{:S(2)}) collective-permute-start(f32[2,48,1152]{2,1,0:T(8,128)S(1)} %slice.168), channel_id=1, source_target_pairs={{0,16},{2,18},{4,20},{6,22},{8,24},{10,26},{12,28},{14,30},{16,0},... | collective-permute-start | bytes 1327112 | tf_op jit(solution)/shard_map/ppermute | solution.py:50
  (123 other events, 1630.4 us)

commit v3 on v2

--- a/solution.py
+++ b/solution.py
@@ -13,6 +13,7 @@
 bfloat = jnp.bfloat16
 single = jnp.float32
 MIB = 1 << 20
+COST_UNIT = 0.5e9
 
 
 def dot(left, right):
@@ -29,21 +30,61 @@
     return jax.ShapeDtypeStruct(shape, dtype)
 
 
-def call(kernel, outs, *args, scalars=(), scratch=(), grid=(), in_specs=None, out_specs=None, limit=48):
-    many = isinstance(outs, (tuple, list))
-    if in_specs is None:
-        in_specs = [pl.BlockSpec(memory_space=pltpu.VMEM)] * len(args)
-        out_specs = [pl.BlockSpec(memory_space=pltpu.VMEM)] * len(outs) if many else pl.BlockSpec(memory_space=pltpu.VMEM)
-    return pl.pallas_call(
-        kernel,
-        out_shape=outs,
-        grid=grid,
-        in_specs=[pl.BlockSpec(memory_space=pltpu.SMEM)] * len(scalars) + list(in_specs),
-        out_specs=out_specs,
-        scratch_shapes=list(scratch),
-        compiler_params=pltpu.CompilerParams(vmem_limit_bytes=limit * MIB),
-        cost_estimate=pl.CostEstimate(flops=1000, bytes_accessed=1000, transcendentals=0),
-    )(*scalars, *args)
+class Order:
+    def __init__(self):
+        self.last = None
+
+    def call(self, kernel, outs, *args, scalars=(), scratch=(), grid=(), in_specs=None, out_specs=None, limit=24, aliases=None, cost=1.0):
+        many = isinstance(outs, (tuple, list))
+        if in_specs is None:
+            in_specs = [pl.BlockSpec(memory_space=pltpu.VMEM)] * len(args)
+        if out_specs is None:
+            out_specs = [pl.BlockSpec(memory_space=pltpu.VMEM)] * len(outs) if many else pl.BlockSpec(memory_space=pltpu.VMEM)
+        in_specs = [pl.BlockSpec(memory_space=pltpu.SMEM)] * len(scalars) + list(in_specs)
+        operands = list(scalars) + list(args)
+        run = kernel
+        if self.last is not None:
+            before = len(operands)
+            operands.append(self.last)
+            in_specs.append(pl.BlockSpec(memory_space=pl.ANY))
+
+            def run(*refs):
+                kernel(*refs[:before], *refs[before + 1 :])
+
+        made = pl.pallas_call(
+            run,
+            out_shape=outs,
+            grid=grid,
+            in_specs=in_specs,
+            out_specs=out_specs,
+            scratch_shapes=list(scratch),
+            input_output_aliases=aliases or {},
+            compiler_params=pltpu.CompilerParams(vmem_limit_bytes=limit * MIB),
+            cost_estimate=pl.CostEstimate(flops=int(cost * COST_UNIT), bytes_accessed=1000, transcendentals=0),
+        )(*operands)
+        self.last = made[-1] if many else made
+        return made
+
+    def pin(self, value):
+        return self.call(
+            lambda *refs: None,
+            shaped(value.shape, value.dtype),
+            value,
+            in_specs=[pl.BlockSpec(memory_space=pl.ANY)],
+            out_specs=pl.BlockSpec(memory_space=pl.ANY),
+            aliases={0: 0},
+            cost=0.0,
+        )
+
+
+class Chain:
+    def __init__(self, steps):
+        self.steps = steps
+        self.value = None
+
+    def step(self):
+        self.value = next(self.steps, self.value)
+        return self.value
 
 
 def swap_dp(value, mask, size):
@@ -75,7 +116,7 @@
             at += 1
 
 
-def place(parts, shape):
+def place(order, parts, shape):
     pieces, rows, starts = [], [], []
     for held, begin in parts:
         pieces += held
@@ -83,38 +124,42 @@
         rows += [held[0].shape[-2]] * len(begin)
     groups = tuple(piece.shape[0] for piece in pieces)
     kernel = functools.partial(place_kernel, groups, tuple(rows))
-    return call(kernel, shaped(shape, bfloat), *pieces, scalars=(jnp.stack(starts),))
-
-
-def fetch_spread(own, me, size, masks, base=0):
-    masks = [mask for mask in masks if mask < size]
-    count = 2 << len(masks)
-    rank = me & (count - 1)
-    rows = own.shape[-2] // count
+    return order.call(kernel, shaped(shape, bfloat), *pieces, scalars=(jnp.stack(starts),), cost=2.4)
+
+
+def pack_kernel(first_ref, second_ref, out_ref):
+    out_ref[0] = first_ref[0]
+    out_ref[1] = second_ref[0]
+
+
+def fetch_spread(order, own, me, size, masks, base=0):
+    first, second = masks
+    rank = me & 7
+    rows = own.shape[-2] // 8
     held = lax.dynamic_slice_in_dim(own, rank * rows, rows, axis=own.ndim - 2).astype(single)
-    pieces = [swap_x(held)[None]]
-    offsets = [[0]]
-    for mask in masks:
-        whole = pieces[0] if len(pieces) == 1 else jnp.concatenate(pieces, axis=0)
-        flat = [o for part in offsets for o in part]
-        pieces = [whole, swap_dp(whole, mask, size)]
-        offsets = [flat, [o ^ mask for o in flat]]
-    pieces = pieces + [swap_dp(piece, 1, size) for piece in pieces]
-    flat = [o for part in offsets for o in part]
-    flat = flat + [o ^ 1 for o in flat]
-    return pieces, [base + (rank ^ o) * rows for o in flat]
-
-
-def fetch_direct(own, me, size, base=0):
+    held = swap_x(held[None])
+    yield
+    held = order.pin(held)
+    arrived = swap_dp(held, first, size)
+    yield
+    both = order.call(pack_kernel, shaped((2,) + held.shape[1:], single), held, arrived, cost=2.0)
+    arrived = swap_dp(both, second, size)
+    both_core = swap_dp(both, 1, size)
+    yield
+    arrived = order.pin(arrived)
+    arrived_core = swap_dp(arrived, 1, size)
+    offsets = [0, first, second, first ^ second]
+    offsets = offsets + [o ^ 1 for o in offsets]
+    yield [both, arrived, both_core, arrived_core], [base + (rank ^ o) * rows for o in offsets]
+
+
+def fetch_direct(order, own, me, size, base=0):
     rows = own.shape[0] // 2
     core = me & 1
-    held = swap_x(lax.dynamic_slice_in_dim(own, core * rows, rows).astype(single))[None]
-    return [held, swap_dp(held, 1, size)], [base + core * rows, base + (1 - core) * rows]
-
-
-def halve(value, mask, size):
-    middle = value.shape[-2] // 2
-    return value[..., :middle, :] + swap_dp(value[..., middle:, :], mask, size)
+    held = swap_x(lax.dynamic_slice_in_dim(own, core * rows, rows).astype(single)[None])
+    yield
+    held = order.pin(held)
+    yield [held, swap_dp(held, 1, size)], [base + core * rows, base + (1 - core) * rows]
 
 
 def sum_all(value, size):
@@ -123,96 +168,101 @@
     return value
 
 
-def grad_kernel(sides, terms, split, *refs):
+def product_kernel(sides, terms, cuts, *refs):
     left_ref = refs[0]
     rights = refs[1 : 1 + sides]
     added = refs[1 + sides : 1 + sides + terms]
     outs = refs[1 + sides + terms :]
-
-    def step(right_ref):
+    parts = len(outs)
+    for s, right_ref in enumerate(rights):
         total = dot(left_ref[...], right_ref[...])
         for term in added:
-            total = total + term[...].reshape(total.shape)
-        if split:
-            middle = total.shape[0] // 2
-            outs[0][...] = total[:middle].reshape(outs[0].shape)
-            outs[1][...] = total[middle:].reshape(outs[1].shape)
-        else:
-            outs[0][...] = total.reshape(outs[0].shape)
-
-    if sides == 1:
-        step(rights[0])
-    else:
-        pl.when(pl.program_id(0) == 0)(lambda: step(rights[0]))
-        pl.when(pl.program_id(0) == 1)(lambda: step(rights[1]))
-
-
-def grad_part(left, half, rights, added=(), split=False):
+            total = total + term[s]
+        height = total.shape[0] // parts
+        for k, out_ref in enumerate(outs):
+            out_ref[s] = total[k * height : (k + 1) * height]
+
+
+def product(order, left, half, rights, added=(), parts=1):
     depth, tokens = left.shape
     rows = depth // 2
-    width = rights[0].shape[1]
-    tile = 512 if width % 512 == 0 else 384
-    steps = width // tile
+    width = rights[0][2]
+    tile = 384 if width % 384 == 0 else 128
     sides = len(rights)
-    if sides == 1:
-        grid = (steps,)
-        right_specs = [pl.BlockSpec((tokens, tile), lambda j: (0, j))]
-        left_spec = pl.BlockSpec((rows, tokens), lambda j: (half, 0))
-
-        def block(height):
-            return pl.BlockSpec((height, tile), lambda j: (0, j))
-
-        def full(height):
-            return (height, width)
-    else:
-        grid = (2, steps)
-        right_specs = [
-            pl.BlockSpec((tokens, tile), lambda s, j: (0, jnp.where(s == 0, j, steps - 1))),
-            pl.BlockSpec((tokens, tile), lambda s, j: (0, jnp.where(s == 0, 0, j))),
-        ]
-        left_spec = pl.BlockSpec((rows, tokens), lambda s, j: (half, 0))
-
-        def block(height):
-            return pl.BlockSpec((1, height, tile), lambda s, j: (s, 0, j))
-
-        def full(height):
-            return (2, height, width)
-
-    heights = (rows // 2, rows // 2) if split else (rows,)
-    outs = call(
-        functools.partial(grad_kernel, sides, len(added), split),
-        [shaped(full(height), single) for height in heights],
+
+    def right_spec(first):
+        return pl.BlockSpec((tokens, tile), lambda j: (0, j + first // tile))
+
+    def block(height):
+        return pl.BlockSpec((sides, height, tile), lambda j: (0, 0, j))
+
+    outs = order.call(
+        functools.partial(product_kernel, sides, len(added), parts),
+        [shaped((sides, rows // parts, width), single)] * parts,
         left,
-        *rights,
+        *[right[0] for right in rights],
         *added,
-        grid=grid,
-        in_specs=[left_spec, *right_specs, *[block(rows) for _ in added]],
-        out_specs=[block(height) for height in heights],
-        limit=32,
-    )
-    return outs if split else outs[0]
-
-
-def finish(low, high, size):
-    total = low + swap_dp(high, 2, size)
-    for k in range(2, size.bit_length() - 1):
-        total = halve(total, 1 << k, size)
-    return total
-
-
-def scatter_x_first(left, own, other, size):
-    other_in = swap_dp(grad_part(left, 1, [other]), 1, size)
-    own_in = swap_dp(grad_part(left, 1, [own]), 1, size)
-    across = swap_x(grad_part(left, 0, [other], [other_in]))
-    low, high = grad_part(left, 0, [own], [own_in, across], split=True)
-    return finish(low, high, size)
-
-
-def scatter_y_first(left, own, other, size):
-    arrived = swap_dp(grad_part(left, 1, [own, other]), 1, size)
-    low, high = grad_part(left, 0, [own, other], [arrived], split=True)
-    total = finish(low, high, size)
-    return total[0] + swap_x(total[1])
+        grid=(width // tile,),
+        in_specs=[
+            pl.BlockSpec((rows, tokens), lambda j: (half, 0)),
+            *[right_spec(right[1]) for right in rights],
+            *[block(rows) for _ in added],
+        ],
+        out_specs=[block(rows // parts)] * parts,
+        cost=sides * width / 1024,
+    )
+    return outs
+
+
+def sum_kernel(parts, first_ref, second_ref, *outs):
+    if first_ref.shape == outs[0].shape:
+        outs[0][...] = first_ref[...] + second_ref[...]
+        return
+    height = first_ref.shape[1] // 2
+    for k in range(2):
+        outs[k][...] = first_ref[:, k * height : (k + 1) * height] + second_ref[:, k * height : (k + 1) * height]
+
+
+def add_split(order, first, second):
+    sides, rows, width = first.shape
+    half = shaped((sides, rows // 2, width), single)
+    return order.call(functools.partial(sum_kernel, 2), [half, half], first, second, cost=0.7)
+
+
+def add_whole(order, first, second):
+    return order.call(functools.partial(sum_kernel, 1), shaped(first.shape, single), first, second, cost=0.5)
+
+
+def scatter_x_first(order, left, own, other, size):
+    (sent,) = product(order, left, 1, [other, own])
+    arrived = swap_dp(sent, 1, size)
+    yield
+    (across,) = product(order, left, 0, [other], [arrived])
+    across = swap_x(across)
+    yield
+    low, high = product(order, left, 0, [own], [arrived[1:], across], parts=2)
+    for k in range(1, size.bit_length() - 1):
+        arrived = swap_dp(high, 1 << k, size)
+        yield
+        if k + 2 < size.bit_length():
+            low, high = add_split(order, low, arrived)
+    yield add_whole(order, low, arrived)[0]
+
+
+def scatter_y_first(order, left, own, other, size):
+    (sent,) = product(order, left, 1, [own, other])
+    arrived = swap_dp(sent, 1, size)
+    yield
+    low, high = product(order, left, 0, [own, other], [arrived], parts=2)
+    for k in range(1, size.bit_length() - 1):
+        arrived = swap_dp(high, 1 << k, size)
+        yield
+        if k + 2 < size.bit_length():
+            low, high = add_split(order, low, arrived)
+    total = add_whole(order, low, arrived)
+    arrived = swap_x(total[1:])
+    yield
+    yield add_whole(order, total[:1], arrived)[0]
 
 
 def relative_kernel(value_ref, source_ref, out_ref):
@@ -229,8 +279,8 @@
     lax.fori_loop(0, 4, step, 0)
 
 
-def relative(value, source):
-    return call(relative_kernel, shaped(value.shape[::-1], bfloat), value, source)
+def relative(order, value, source):
+    return order.call(relative_kernel, shaped(value.shape[::-1], bfloat), value, source, cost=1.7)
 
 
 def attend_kernel(length_ref, rows_ref, qkv_ref, bias_ref, out_w_ref, start_ref, parts_ref, chance_ref, context_ref, hidden_ref, turned_ref):
@@ -272,10 +322,10 @@
     hidden_ref[...] = start_ref[...] + dot(context, out_w_ref[...])
 
 
-def attend(length, rows, qkv, bias, out, start):
+def attend(order, length, rows, qkv, bias, out, start):
     tokens, width = rows.shape
     local = qkv.shape[2]
-    return call(
+    return order.call(
         attend_kernel,
         [
             shaped((3, tokens, local), bfloat),
@@ -290,6 +340,7 @@
         start,
         scalars=(length,),
         scratch=[pltpu.VMEM((local, tokens), bfloat)],
+        cost=9.0,
     )
 
 
@@ -354,10 +405,10 @@
     hidden_ref[...] = start_ref[...] + dot(act_ref[...], down_ref[...])
 
 
-def feed(normed, into, bias, down, start):
+def feed(order, normed, into, bias, down, start):
     tokens, width = normed.shape
     units = into.shape[1]
-    return call(
+    return order.call(
         feed_kernel,
         [shaped((tokens, units), bfloat), shaped((tokens, units), bfloat), shaped((tokens, width), single)],
         normed,
@@ -365,6 +416,7 @@
         bias,
         down,
         start,
+        cost=6.0,
     )
 
 
@@ -372,7 +424,7 @@
     ref[row : row + 1, :] += jnp.sum(value, axis=0, keepdims=True)
 
 
-def turn_kernel(hidden_ref, gain_ref, shift_ref, upstream_ref, unit_ref, result_ref, grad_ref, branch_ref, sums_ref):
+def turn_kernel(hidden_ref, gain_ref, shift_ref, upstream_ref, result_ref, grad_ref, sums_ref, unit_ref, branch_ref):
     sums_ref[...] = jnp.zeros_like(sums_ref)
 
     def body(at):
@@ -407,10 +459,10 @@
     normed_ref[...] = start_ref[...] + dot_cols(grad_ref[...], into_ref[...])
 
 
-def feed_back(branch, down, slope, into, start):
+def feed_back(order, branch, down, slope, into, start):
     tokens, width = branch.shape
     units = into.shape[1]
-    return call(
+    return order.call(
         feed_back_kernel,
         [shaped((tokens, units), bfloat), shaped((1, units), single), shaped((tokens, width), single)],
         branch,
@@ -418,10 +470,11 @@
         slope,
         into,
         start,
-    )
-
-
-def norm_back_kernel(hidden_ref, gain_ref, upstream_ref, grad_ref, low_ref, sums_ref):
+        cost=3.9,
+    )
+
+
+def norm_back_kernel(hidden_ref, gain_ref, upstream_ref, grad_ref, sums_ref, low_ref):
     sums_ref[...] = jnp.zeros_like(sums_ref)
 
     def body(at):
@@ -487,10 +540,10 @@
     rows_ref[...] = total
 
 
-def attend_back(upstream, out, parts, chances, qkv, start):
+def attend_back(order, upstream, out, parts, chances, qkv, start):
     tokens, width = upstream.shape
     local = out.shape[0]
-    return call(
+    return order.call(
         attend_back_kernel,
         [shaped((tokens, 3 * local), bfloat), shaped((1, 3 * local), single), shaped((tokens, width), single)],
         upstream,
@@ -500,7 +553,53 @@
         qkv,
         start,
         scratch=[pltpu.VMEM((local, tokens), bfloat)],
-    )
+        cost=9.4,
+    )
+
+
+def vectors_kernel(first_ref, second_ref, units_own, units_other, proj_own, proj_other, own_ref, other_ref):
+    width = first_ref.shape[1]
+    local = proj_own.shape[1] // 3
+    for units, proj, out in ((units_own, proj_own, own_ref), (units_other, proj_other, other_ref)):
+        out[...] = jnp.zeros_like(out)
+        out[0:3, :] = first_ref[...]
+        out[3:6, :] = second_ref[...]
+        for k in range(units.shape[1] // width):
+            out[6 + k : 7 + k, :] = units[:, k * width : (k + 1) * width]
+        row = 6 + units.shape[1] // width
+        out[row : row + 1, 0:local] = proj[:, 0:local]
+        out[row : row + 1, local : 2 * local] = proj[:, 2 * local :]
+
+
+def sum_vectors(order, own, other, size):
+    arrived = swap_x(other)
+    yield
+    total = order.call(vector_add_kernel, shaped(own.shape, single), own, arrived, cost=0.1)
+    for k in range(size.bit_length() - 1):
+        arrived = swap_dp(total, 1 << k, size)
+        yield
+        total = order.call(vector_add_kernel, shaped(own.shape, single), total, arrived, cost=0.1)
+    yield total
+
+
+def vector_add_kernel(first_ref, second_ref, out_ref):
+    out_ref[...] = first_ref[...] + second_ref[...]
+
+
+def both_result_kernel(side_ref, mine_ref, unit_ref, gain_ref, shift_ref, out_ref):
+    side = side_ref[0]
+    out_ref[side] = mine_ref[...]
+
+    def body(at):
+        out_ref[1 - side, at, :] = (unit_ref[at, :] * gain_ref[1:2, :] + shift_ref[1:2, :]).astype(bfloat)
+
+    strips(mine_ref.shape[0], body)
+
+
+def both_kernel(side_ref, mine_ref, other_ref, out_ref):
+    side = side_ref[0]
+    out_ref[side] = mine_ref[...]
+    out_ref[1 - side] = other_ref[...]
 
 
 def body(
@@ -521,6 +620,7 @@
     size = lax.axis_size("dp")
     me = lax.axis_index("dp")
     side = lax.axis_index("tensor")
+    side_index = side.astype(jnp.int32).reshape(1)
     tokens, width = inputs.shape[1:]
     local = w_qkv.shape[2]
     units = w_in.shape[1]
@@ -528,37 +628,51 @@
     length = lax.dynamic_slice_in_dim(lengths, side, 1)
     upstream = lax.dynamic_index_in_dim(cotangent, side, 0, keepdims=False)
 
-    qkv_own = jnp.transpose(w_qkv, (1, 0, 2))
-    small_other = swap_x(jnp.concatenate([b_qv.reshape(-1), b_in]))
-    b_qv_other, b_in_other = small_other[: 2 * local].reshape(2, local), small_other[2 * local :]
-    qkv_other = place([fetch_spread(qkv_own, me, size, (4, 2))], qkv_own.shape)
-    out_other = place([fetch_direct(w_out, me, size)], w_out.shape)
-    in_other = place([fetch_spread(w_in, me, size, (2, 4))], w_in.shape)
-    cut, end = units // 2, 3 * units // 4
-    down_other = place(
-        [
-            fetch_spread(w_down[:cut], me, size, (4, 2)),
-            fetch_spread(w_down[cut:end], me, size, (2, 4), base=cut),
-            fetch_direct(w_down[end:], me, size, base=end),
-        ],
-        w_down.shape,
-    )
-    sides = (
-        (qkv_own, b_qv, w_out, w_in, b_in.reshape(1, -1), w_down),
-        (qkv_other, b_qv_other, out_other, in_other, b_in_other.reshape(1, -1), down_other),
-    )
+    order = Order()
 
     bits = size.bit_length() - 1
     share = width // size
     block_of = jnp.array([reverse_bits(p, bits) for p in range(size)], jnp.int32) ^ me
     source = (block_of[:, None] * share + jnp.arange(share)[None, :]).reshape(-1, 1)
 
+    qkv_own = jnp.transpose(w_qkv, (1, 0, 2))
+    cut = width // 2
+    middle = units // 2
+    get_qkv = fetch_spread(order, qkv_own, me, size, (4, 2))
+    get_in_z = fetch_spread(order, w_in[:cut], me, size, (4, 2))
+    get_in_y = fetch_spread(order, w_in[cut:], me, size, (2, 4), base=cut)
+    get_down_y = fetch_spread(order, w_down[:middle], me, size, (2, 4))
+    get_out = fetch_direct(order, w_out, me, size)
+    get_down_x = fetch_direct(order, w_down[middle:], me, size, base=middle)
+    for chain in (get_qkv, get_in_z, get_in_y, get_down_y, get_out, get_down_x):
+        next(chain)
+    small_other = swap_x(jnp.concatenate([b_qv.reshape(-1), b_in]))
+    b_qv_other, b_in_other = small_other[: 2 * local].reshape(2, local), small_other[2 * local :]
+
     heads = []
     hidden_one = rows.astype(single) + b_out
-    for qkv, bias, out, _, _, _ in sides:
-        parts, chances, context, hidden_one = attend(length, rows, qkv, bias, out, hidden_one)
-        heads.append((parts, chances, context))
-    normed_low, hidden_two = call(
+    parts, chances, context, hidden_one = attend(order, length, rows, qkv_own, b_qv, w_out, hidden_one)
+    heads.append((parts, chances, context))
+    next(get_qkv)
+    next(get_in_z)
+    next(get_in_y)
+    next(get_qkv)
+    next(get_down_y)
+    next(get_in_y)
+    next(get_in_z)
+    parts_out = next(get_out)
+    rows_rel = relative(order, rows, source)
+    parts_qkv = next(get_qkv)
+    parts_in_y = next(get_in_y)
+    out_other = place(order, [parts_out], w_out.shape)
+    qkv_other = place(order, [parts_qkv], qkv_own.shape)
+    next(get_down_y)
+    parts, chances, context, hidden_one = attend(order, length, rows, qkv_other, b_qv_other, out_other, hidden_one)
+    heads.append((parts, chances, context))
+    parts_in_z = next(get_in_z)
+    parts_down_y = next(get_down_y)
+    parts_down_x = next(get_down_x)
+    normed_low, hidden_two = order.call(
         norm_kernel,
         [shaped((tokens, width), bfloat), shaped((tokens, width), single)],
         hidden_one,
@@ -567,83 +681,133 @@
         b_down.reshape(1, -1),
     )
     acts = []
-    for _, _, _, into, bias, down in sides:
-        act, slope, hidden_two = feed(normed_low, into, bias, down, hidden_two)
-        acts.append((act, slope))
-    unit_two, result, grad_two, branch, sums_two = call(
+    act, slope, hidden_two = feed(order, normed_low, w_in, b_in.reshape(1, -1), w_down, hidden_two)
+    acts.append((act, slope))
+    normed_rel = relative(order, normed_low, source)
+    in_other = place(order, [parts_in_z, parts_in_y], w_in.shape)
+    down_other = place(order, [parts_down_y, parts_down_x], w_down.shape)
+    act, slope, hidden_two = feed(order, normed_low, in_other, b_in_other.reshape(1, -1), down_other, hidden_two)
+    acts.append((act, slope))
+    result, grad_two, sums_two, unit_two, branch = order.call(
         turn_kernel,
         [
+            shaped((tokens, width), bfloat),
+            shaped((tokens, width), single),
+            shaped((3, width), single),
             shaped((tokens, width), single),
             shaped((tokens, width), bfloat),
-            shaped((tokens, width), single),
-            shaped((tokens, width), bfloat),
-            shaped((3, width), single),
         ],
         hidden_two,
         ln_gains,
         ln_biases,
         upstream,
     )
-    result_other = (swap_x(unit_two) * ln_gains[1] + ln_biases[1]).astype(bfloat)
-
-    share_down = scatter_x_first(relative(branch, source), acts[0][0], acts[1][0], size)
-    grad_pres, unit_sums = [], []
-    grad_normed = grad_two
-    for (_, slope), (_, _, _, into, _, down) in zip(acts, sides):
-        grad_pre, unit_sum, grad_normed = feed_back(branch, down, slope, into, grad_normed)
-        grad_pres.append(grad_pre)
-        unit_sums.append(unit_sum)
-    share_in = scatter_y_first(relative(normed_low, source), grad_pres[0], grad_pres[1], size)
-    grad_one, attended, sums_one = call(
+
+    half = units // 2
+    branch_rel = relative(order, branch, source)
+    down_x = Chain(scatter_x_first(order, branch_rel, (acts[0][0], 0, half), (acts[1][0], 0, half), size))
+    down_y = Chain(scatter_y_first(order, branch_rel, (acts[0][0], half, half), (acts[1][0], half, half), size))
+    down_x.step()
+    down_y.step()
+    unit_other = swap_x(unit_two)
+    pre_other, unit_sum_other, grad_normed = feed_back(order, branch, down_other, acts[1][1], in_other, grad_two)
+    down_x.step()
+    pre_own, unit_sum_own, grad_normed = feed_back(order, branch, w_down, acts[0][1], w_in, grad_normed)
+    down_y.step()
+    in_y = Chain(scatter_y_first(order, normed_rel, (pre_own, half, half), (pre_other, half, half), size))
+    in_x = Chain(scatter_x_first(order, normed_rel, (pre_own, 0, half), (pre_other, 0, half), size))
+    in_x.step()
+    in_y.step()
+    grad_one, sums_one, attended = order.call(
         norm_back_kernel,
-        [shaped((tokens, width), single), shaped((tokens, width), bfloat), shaped((3, width), single)],
+        [shaped((tokens, width), single), shaped((3, width), single), shaped((tokens, width), bfloat)],
         hidden_one,
         ln_gains,
         grad_normed,
     )
-    share_out = scatter_x_first(relative(attended, source), heads[0][2], heads[1][2], size)
+    attended_rel = relative(order, attended, source)
+    out_x = Chain(scatter_x_first(order, attended_rel, (heads[0][2], 0, local), (heads[1][2], 0, local), size))
+    out_x.step()
+    in_x.step()
+    down_x.step()
+    in_y.step()
+    out_x.step()
     grad_rows = grad_one
-    grad_projs, proj_sums = [], []
-    for (parts, chances, _), (qkv, _, out, _, _, _) in zip(heads, sides):
-        grad_proj, proj_sum, grad_rows = attend_back(attended, out, parts, chances, qkv, grad_rows)
-        grad_projs.append(grad_proj)
-        proj_sums.append(proj_sum)
+    proj_other, proj_sum_other, grad_rows = attend_back(order, attended, out_other, heads[1][0], heads[1][1], qkv_other, grad_rows)
+    down_y.step()
+    down_x.step()
+    proj_own, proj_sum_own, grad_rows = attend_back(order, attended, w_out, heads[0][0], heads[0][1], qkv_own, grad_rows)
+    cut = 768 if local == 384 else local
+    last = 3 * local
+    qkv_x = Chain(scatter_x_first(order, rows_rel, (proj_own, 0, cut), (proj_other, 0, cut), size))
+    qkv_y = Chain(scatter_y_first(order, rows_rel, (proj_own, cut, last - cut), (proj_other, cut, last - cut), size))
+    own_vectors, other_vectors = order.call(
+        vectors_kernel,
+        [shaped((16, width), single)] * 2,
+        sums_one,
+        sums_two,
+        unit_sum_own,
+        unit_sum_other,
+        proj_sum_own,
+        proj_sum_other,
+        cost=0.5,
+    )
+    vectors = Chain(sum_vectors(order, own_vectors, other_vectors, size))
+    qkv_x.step()
+    qkv_y.step()
     grad_rows_other = swap_x(grad_rows)
-    share_qkv = scatter_y_first(relative(rows, source), grad_projs[0], grad_projs[1], size)
-
-    every = jnp.concatenate([sums_one.reshape(-1), sums_two.reshape(-1)])
-    vectors = jnp.concatenate([every, unit_sums[0].reshape(-1)])
-    vectors_other = swap_x(jnp.concatenate([every, unit_sums[1].reshape(-1)]))
-    vectors = sum_all(vectors + vectors_other, size)
-    qv_own, qv_other = (
-        jnp.concatenate([part[0, :local], part[0, 2 * local :]]) for part in proj_sums
-    )
-    grad_b_qv = sum_all(qv_own + swap_x(qv_other), size).reshape(2, local)
-    gain_one, shift_one, b_out_g, gain_two, shift_two, b_down_g = (
-        vectors[k * width : (k + 1) * width] for k in range(6)
-    )
-
-    def both(mine, other):
-        mine, other = mine[None], other[None]
-        return jnp.where(
-            side == 0,
-            jnp.concatenate([mine, other], axis=0),
-            jnp.concatenate([other, mine], axis=0),
-        )
+    in_x.step()
+    down_y.step()
+    down_x.step()
+    out_x.step()
+    results = order.call(
+        both_result_kernel,
+        shaped((2, tokens, width), bfloat),
+        result,
+        unit_other,
+        ln_gains,
+        ln_biases,
+        scalars=(side_index,),
+        cost=1.5,
+    )
+    vectors.step()
+    qkv_x.step()
+    qkv_y.step()
+    in_y.step()
+    chains = (down_x, in_x, out_x, down_y, in_y, qkv_x, qkv_y, vectors)
+    while any(chain.value is None for chain in chains):
+        for chain in chains:
+            if chain.value is None:
+                chain.step()
+    grads = order.call(
+        both_kernel,
+        shaped((2, tokens, width), single),
+        grad_rows,
+        grad_rows_other,
+        scalars=(side_index,),
+        cost=2.0,
+    )
+    share_down = jnp.concatenate([down_x.value, down_y.value], axis=1)
+    share_in = jnp.concatenate([in_x.value, in_y.value], axis=1)
+    share_qkv = jnp.concatenate([qkv_x.value, qkv_y.value], axis=1)
+
+    total = vectors.value
+    grad_b_in = total[6 : 6 + units // width].reshape(-1)
+    grad_b_qv = total[6 + units // width].reshape(2, local)
 
     return (
-        both(result, result_other),
-        both(grad_rows, grad_rows_other),
+        results,
+        grads,
         share_qkv.reshape(-1, 3, local),
         grad_b_qv,
-        share_out.T,
-        b_out_g,
-        jnp.stack([gain_one, gain_two]),
-        jnp.stack([shift_one, shift_two]),
+        out_x.value.T,
+        total[2],
+        jnp.stack([total[0], total[3]]),
+        jnp.stack([total[1], total[4]]),
         share_in,
-        vectors[6 * width :],
+        grad_b_in,
         share_down.T,
-        b_down_g,
+        total[5],
     )
 
 

time: 551 us -> 434 us (0.79)
  waiting for transfers between devices: 270 us -> 195 us
  other arithmetic: 30.1 us -> 9.94 us
  Pallas kernels: 139 us -> 119 us
  local copies, waits for them, and re-layouts: 45.7 us -> 34.9 us
    ppermute x44 -> x50, waiting for transfers between devices: 193 us -> 92.5 us  [swap_dp(): return lax.ppermute(value, 'dp', [(i, i ^ mask) for i in range(size)])]
    ppermute x15 -> x17, waiting for transfers between devices: 77 us -> 103 us  [swap_x(): return lax.ppermute(value, 'tensor', [(0, 1), (1, 0)])]
    pallas_call x31 -> x83, Pallas kernels: 139 us -> 119 us  [call(): pl.pallas_call(run, out_shape=outs, grid=grid, in_specs=in_specs, out_spe...]
    unnamed x172 -> x110, local copies, waits for them, and re-layouts: 32.6 us -> 22.3 us
    add x22 -> x0, other arithmetic: 6.64 us -> none  [the longest x4 3.86 us: finish(): total = low + swap_dp(high, 2, size)]
    select_n x2 -> x0, other arithmetic: 6.58 us -> none  [both(): jnp.where(side == 0, jnp.concatenate([mine, other], axis=0), jnp.concaten...]
    ppermute x44 -> x50, starting transfers between devices: 41.6 us -> 47.1 us  [swap_dp(): return lax.ppermute(value, 'dp', [(i, i ^ mask) for i in range(size)])]
    ppermute x15 -> x17, starting transfers between devices: 21 us -> 20 us  [swap_x(): return lax.ppermute(value, 'tensor', [(0, 1), (1, 0)])]
  transfers between devices with their start and end apart: 59 -> 67, of which waited for: 23 -> 19; matrix products, arithmetic and copies ran while one was open for 7% -> 5% of each run, Pallas kernels for 19% -> 20%
where the time goes in v3:
time: 434 us; the launch traced here: 429 us
  waiting for transfers between devices  195 us (45%)
  Pallas kernels  119 us (27%)
  starting transfers between devices  67.1 us (15%)
  local copies, waits for them, and re-layouts  34.9 us (8%)
  other arithmetic  9.94 us (2%)
    pallas_call x83, Pallas kernels, call(): pl.pallas_call(run, out_shape=outs, grid=grid, in_specs=in_specs, out_spe...  119 us
    ppermute x17, waiting for transfers between devices, swap_x(): return lax.ppermute(value, 'tensor', [(0, 1), (1, 0)])  103 us
    ppermute x50, waiting for transfers between devices, swap_dp(): return lax.ppermute(value, 'dp', [(i, i ^ mask) for i in range(size)])  92.5 us
    ppermute x50, starting transfers between devices, swap_dp(): return lax.ppermute(value, 'dp', [(i, i ^ mask) for i in range(size)])  47.1 us
    unnamed x110, local copies, waits for them, and re-layouts  22.3 us
    ppermute x17, starting transfers between devices, swap_x(): return lax.ppermute(value, 'tensor', [(0, 1), (1, 0)])  20 us
  transfers between devices with their start and end apart: 67, of which 19 were waited for; matrix products, arithmetic and copies ran while one was open for 5% of the time, Pallas kernels for 20%

profile of v3, /device:TPU:0, one launch (start us, length us, event | category | flops | bytes accessed | tf_op | source)
XLA Modules:
  0.0 428.5 jit_solution(7889723196140902594)
XLA Ops:
  11.2 8.9 %shard_map.229 = (bf16[3,512,384]{2,1,0:T(8,128)(2,1)S(1)}, bf16[6,512,512]{2,1,0:T(8,128)(2,1)S(1)}, bf16[512,384]{1,0:T(8,128)(2,1)S(1)}, f32[512,768]{1,0:T(8,128)S(1)}) custom-call(s32[1]{0:T(128)} %dynamic_slice.28.length_ref.refs_0_, bf16[512,768]{1,0:T(8,128)(2,1)S(1)} %get-tuple-element.200.rows_ref.refs_0_.refs_1_, ...), custom_call_target="tpu_custom_call" | custom-call | flops 4499999744 | bytes 1000 | tf_op jit(solution)/shard_map/pallas_call | solution.py:54
  29.7 7.1 %collective-permute-done.2.refs_0_ = f32[1,48,1536]{2,1,0:T(8,128)S(1)} collective-permute-done((f32[1,48,1536]{2,1,0:T(8,128)S(1)}, f32[1,48,1536]{2,1,0:T(8,128)S(1)}, u32[]{:S(2)}, u32[]{:S(2)}) %collective-permute-start.2) | collective-permute-done | bytes 294944 | tf_op jit(solution)/shard_map/ppermute | solution.py:95
  45.2 8.5 %collective-permute-done.8.refs_0_ = f32[1,96,768]{2,1,0:T(8,128)S(1)} collective-permute-done((f32[1,96,768]{2,1,0:T(8,128)}, f32[1,96,768]{2,1,0:T(8,128)S(1)}, u32[]{:S(2)}, u32[]{:S(2)}) %collective-permute-start.8) | collective-permute-done | bytes 294944 | tf_op jit(solution)/shard_map/ppermute | solution.py:95
  53.7 10.6 %collective-permute-done.7.refs_1_ = f32[1,48,1536]{2,1,0:T(8,128)S(1)} collective-permute-done((f32[1,48,1536]{2,1,0:T(8,128)S(1)}, f32[1,48,1536]{2,1,0:T(8,128)S(1)}, u32[]{:S(2)}, u32[]{:S(2)}) %collective-permute-start.7) | collective-permute-done | bytes 294944 | tf_op jit(solution)/shard_map/ppermute | solution.py:91
  74.4 11.7 %collective-permute-done.12.refs_0_ = f32[2,48,1536]{2,1,0:T(8,128)} collective-permute-done((f32[2,48,1536]{2,1,0:T(8,128)}, f32[2,48,1536]{2,1,0:T(8,128)}, u32[]{:S(2)}, u32[]{:S(2)}) %collective-permute-start.12) | collective-permute-done | bytes 589856 | tf_op jit(solution)/shard_map/ppermute | solution.py:91
  92.1 4.2 collective-permute-done.14.refs_1_
  108.6 8.9 %shard_map.244 = (bf16[3,512,384]{2,1,0:T(8,128)(2,1)S(1)}, bf16[6,512,512]{2,1,0:T(8,128)(2,1)S(1)}, bf16[512,384]{1,0:T(8,128)(2,1)S(1)}, f32[512,768]{1,0:T(8,128)S(1)}) custom-call(s32[1]{0:T(128)} %dynamic_slice.28.length_ref.refs_0_, bf16[512,768]{1,0:T(8,128)(2,1)S(1)} %copy-done.22, bf16[3,768,384]{2,1,0:T(8,128)(2,1)S(1)} %copy-done.10, ...), custom_call_target="tpu_custom_call" | custom-call | flops 4499999744 | bytes 1000 | tf_op jit(solution)/shard_map/pallas_call | solution.py:54
  129.6 6.0 %shard_map.249 = (bf16[512,1536]{1,0:T(8,128)(2,1)S(1)}, bf16[512,1536]{1,0:T(8,128)(2,1)S(1)}, f32[512,768]{1,0:T(8,128)S(1)}) custom-call(bf16[512,768]{1,0:T(8,128)(2,1)S(1)} %get-tuple-element.94.refs_0_, bf16[768,1536]{1,0:T(8,128)(2,1)S(1)} %copy-done.4, f32[1,1536]{1,0:T(1,128)S(1)} %copy-done.35, bf16[1536,768]{1,0:T(8,128)(2,1)S(1)} %copy-done.6, ...), custom_call_target="tpu_custom_call" | custom-call | flops 3000000000 | bytes 1000 | tf_op jit(solution)/shard_map/pallas_call | solution.py:54
  142.0 6.3 %shard_map.253 = (bf16[512,1536]{1,0:T(8,128)(2,1)S(1)}, bf16[512,1536]{1,0:T(8,128)(2,1)S(1)}, f32[512,768]{1,0:T(8,128)S(1)}) custom-call(bf16[512,768]{1,0:T(8,128)(2,1)S(1)} %get-tuple-element.94.refs_0_, bf16[768,1536]{1,0:T(8,128)(2,1)S(1)} %shard_map.251.refs_7_.refs_1_.refs_3_, f32[1,1536]{1,0:T(1,128)S(1)} %reshape.84.refs_2_, ...), custom_call_target="tpu_custom_call" | custom-call | flops 3000000000 | bytes 1000 | tf_op jit(solution)/shard_map/pallas_call | solution.py:54
  155.3 3.9 shard_map.258
  160.9 3.9 shard_map.260
  178.4 20.1 %collective-permute-done.30.refs_3_ = f32[1,384,768]{2,1,0:T(8,128)S(1)} collective-permute-done((f32[1,384,768]{2,1,0:T(8,128)S(1)}, f32[1,384,768]{2,1,0:T(8,128)S(1)}, u32[]{:S(2)}, u32[]{:S(2)}) %collective-permute-start.30) | collective-permute-done | bytes 1179680 | tf_op jit(solution)/shard_map/ppermute | solution.py:95
  204.9 18.9 %shard_map.271 = (bf16[512,1152]{1,0:T(8,128)(2,1)S(1)}, f32[1,1152]{1,0:T(1,128)S(1)}, f32[512,768]{1,0:T(8,128)S(1)}) custom-call(bf16[512,768]{1,0:T(8,128)(2,1)S(1)} %get-tuple-element.111.refs_0_.refs_2_, bf16[384,768]{1,0:T(8,128)(2,1)S(1)} %copy-done.25, bf16[3,512,384]{2,1,0:T(8,128)(2,1)S(1)} %copy-done.46, bf16[6,512,512]{2,1,0:T(8,128)(2,1)S(1)} %copy-done.42, ...), custom_call_target="tpu_custom_call" | custom-call | flops 4700000256 | bytes 1000 | tf_op jit(solution)/shard_map/pallas_call | solution.py:54
  226.4 10.4 %shard_map.274 = (bf16[512,1152]{1,0:T(8,128)(2,1)S(1)}, f32[1,1152]{1,0:T(1,128)S(1)}, f32[512,768]{1,0:T(8,128)}) custom-call(bf16[512,768]{1,0:T(8,128)(2,1)S(1)} %get-tuple-element.111.refs_0_.refs_2_, bf16[384,768]{1,0:T(8,128)(2,1)S(1)} %copy-done.29, bf16[3,512,384]{2,1,0:T(8,128)(2,1)S(1)} %copy-done.48, bf16[6,512,512]{2,1,0:T(8,128)(2,1)S(1)} %copy-done.44, ...), custom_call_target="tpu_custom_call" | custom-call | flops 4700000256 | bytes 1000 | tf_op jit(solution)/shard_map/pallas_call | solution.py:54
  242.5 14.2 %collective-permute-done.36.refs_1_ = f32[2,96,768]{2,1,0:T(8,128)S(1)} collective-permute-done((f32[2,96,768]{2,1,0:T(8,128)S(1)}, f32[2,96,768]{2,1,0:T(8,128)S(1)}, u32[]{:S(2)}, u32[]{:S(2)}) %collective-permute-start.36) | collective-permute-done | bytes 589856 | tf_op jit(solution)/shard_map/ppermute | solution.py:91
  261.9 5.3 %collective-permute-done.37.refs_3_ = f32[1,384,768]{2,1,0:T(8,128)S(1)} collective-permute-done((f32[1,384,768]{2,1,0:T(8,128)S(1)}, f32[1,384,768]{2,1,0:T(8,128)S(1)}, u32[]{:S(2)}, u32[]{:S(2)}) %collective-permute-start.37) | collective-permute-done | bytes 1179680 | tf_op jit(solution)/shard_map/ppermute | solution.py:95
  269.1 44.0 %collective-permute-done.32.refs_3_ = f32[1,384,384]{2,1,0:T(8,128)S(1)} collective-permute-done((f32[1,384,384]{2,1,0:T(8,128)S(1)}, f32[1,384,384]{2,1,0:T(8,128)S(1)}, u32[]{:S(2)}, u32[]{:S(2)}) %collective-permute-start.32) | collective-permute-done | bytes 589856 | tf_op jit(solution)/shard_map/ppermute | solution.py:95
  324.7 10.9 %collective-permute-done.49.refs_1_ = f32[1,48,768]{2,1,0:T(8,128)S(1)} collective-permute-done((f32[1,48,768]{2,1,0:T(8,128)S(1)}, f32[1,48,768]{2,1,0:T(8,128)S(1)}, u32[]{:S(2)}, u32[]{:S(2)}) %collective-permute-start.49) | collective-permute-done | bytes 147488 | tf_op jit(solution)/shard_map/ppermute | solution.py:91
  341.3 10.6 %collective-permute-done.46.refs_1_ = f32[2,48,768]{2,1,0:T(8,128)S(1)} collective-permute-done((f32[2,48,768]{2,1,0:T(8,128)S(1)}, f32[2,48,768]{2,1,0:T(8,128)S(1)}, u32[]{:S(2)}, u32[]{:S(2)}) %collective-permute-start.46) | collective-permute-done | bytes 294944 | tf_op jit(solution)/shard_map/ppermute | solution.py:91
  358.2 11.0 %collective-permute-done.56.refs_1_ = f32[1,96,768]{2,1,0:T(8,128)S(1)} collective-permute-done((f32[1,96,768]{2,1,0:T(8,128)S(1)}, f32[1,96,768]{2,1,0:T(8,128)S(1)}, u32[]{:S(2)}, u32[]{:S(2)}) %collective-permute-start.56) | collective-permute-done | bytes 294944 | tf_op jit(solution)/shard_map/ppermute | solution.py:91
  374.0 10.2 %collective-permute-done.51.refs_1_ = f32[2,96,384]{2,1,0:T(8,128)S(1)} collective-permute-done((f32[2,96,384]{2,1,0:T(8,128)S(1)}, f32[2,96,384]{2,1,0:T(8,128)S(1)}, u32[]{:S(2)}, u32[]{:S(2)}) %collective-permute-start.51) | collective-permute-done | bytes 294944 | tf_op jit(solution)/shard_map/ppermute | solution.py:91
  392.4 14.3 %collective-permute-done.60.refs_1_ = f32[1,48,768]{2,1,0:T(8,128)S(1)} collective-permute-done((f32[1,48,768]{2,1,0:T(8,128)S(1)}, f32[1,48,768]{2,1,0:T(8,128)S(1)}, u32[]{:S(2)}, u32[]{:S(2)}) %collective-permute-start.60) | collective-permute-done | bytes 147488 | tf_op jit(solution)/shard_map/ppermute | solution.py:95
  417.7 4.2 collective-permute-done.66.refs_1_
  424.4 3.9 shard_map.311
  (345 shorter events, 168.3 us)
Async XLA Ops:
  29.2 37.9 %collective-permute-start.5 = (f32[1,192,768]{2,1,0:T(8,128)}, f32[1,192,768]{2,1,0:T(8,128)}, u32[]{:S(2)}, u32[]{:S(2)}) collective-permute-start(f32[1,192,768]{2,1,0:T(8,128)} %bitcast_convert_fusion.1), channel_id=1, source_target_pairs={{0,1},{1,0},{2,3},{3,2},{4,5},{5,4},{6,7},{7,6},{8,9},{9,8},{10,11... | collective-permute-start | bytes 1769480 | tf_op jit(solution)/shard_map/ppermute | solution.py:95
  39.0 31.0 %collective-permute-start.4 = (f32[2,3,96,384]{3,2,1,0:T(8,128)}, f32[2,3,96,384]{3,2,1,0:T(8,128)}, u32[]{:S(2)}, u32[]{:S(2)}) collective-permute-start(f32[2,3,96,384]{3,2,1,0:T(8,128)} %shard_map.233.refs_1_), channel_id=1, source_target_pairs={{0,4},{2,6},{4,0},{6,2},{8,12},{10,14},{12,8},{14,10},{16,20},{18,... | collective-permute-start | bytes 2654216 | tf_op jit(solution)/shard_map/ppermute | solution.py:91
  53.7 35.9 %collective-permute-start.9 = (f32[2,3,96,384]{3,2,1,0:T(8,128)}, f32[2,3,96,384]{3,2,1,0:T(8,128)}, u32[]{:S(2)}, u32[]{:S(2)}) collective-permute-start(f32[2,3,96,384]{3,2,1,0:T(8,128)} %shard_map.233.refs_1_), channel_id=1, source_target_pairs={{0,2},{2,0},{4,6},{6,4},{8,10},{10,8},{12,14},{14,12},{16,18},{18,... | collective-permute-start | bytes 2654216 | tf_op jit(solution)/shard_map/ppermute | solution.py:91
  72.9 48.1 %collective-permute-start.15 = (f32[1,384,768]{2,1,0:T(8,128)}, f32[1,384,768]{2,1,0:T(8,128)S(1)}, u32[]{:S(2)}, u32[]{:S(2)}) collective-permute-start(f32[1,384,768]{2,1,0:T(8,128)} %bitcast_convert_fusion), channel_id=1, source_target_pairs={{0,1},{1,0},{2,3},{3,2},{4,5},{5,4},{6,7},{7,6},{8,9},{9,8},{10,11... | collective-permute-start | bytes 3538952 | tf_op jit(solution)/shard_map/ppermute | solution.py:95
  87.6 31.6 %collective-permute-start.17 = (f32[2,48,1536]{2,1,0:T(8,128)}, f32[2,48,1536]{2,1,0:T(8,128)}, u32[]{:S(2)}, u32[]{:S(2)}) collective-permute-start(f32[2,48,1536]{2,1,0:T(8,128)} %shard_map.236.refs_1_), channel_id=1, source_target_pairs={{0,4},{2,6},{4,0},{6,2},{8,12},{10,14},{12,8},{14,10},{16,20},{18,... | collective-permute-start | bytes 1769480 | tf_op jit(solution)/shard_map/ppermute | solution.py:91
  97.1 22.1 %collective-permute-start.16 = (f32[2,96,768]{2,1,0:T(8,128)}, f32[2,96,768]{2,1,0:T(8,128)}, u32[]{:S(2)}, u32[]{:S(2)}) collective-permute-start(f32[2,96,768]{2,1,0:T(8,128)} %shard_map.243.refs_6_.refs_1_), channel_id=1, source_target_pairs={{0,8},{2,10},{4,12},{6,14},{8,0},{10,2},{12,4},{14,6},{16,24},{18,... | collective-permute-start | bytes 1769480 | tf_op jit(solution)/shard_map/ppermute | solution.py:91
  103.0 22.5 %collective-permute-start.18 = (f32[2,48,1536]{2,1,0:T(8,128)}, f32[2,48,1536]{2,1,0:T(8,128)}, u32[]{:S(2)}, u32[]{:S(2)}) collective-permute-start(f32[2,48,1536]{2,1,0:T(8,128)} %shard_map.236.refs_1_), channel_id=1, source_target_pairs={{0,2},{2,0},{4,6},{6,4},{8,10},{10,8},{12,14},{14,12},{16,18},{18,... | collective-permute-start | bytes 1769480 | tf_op jit(solution)/shard_map/ppermute | solution.py:91
  103.0 22.9 %collective-permute-start.20 = (f32[2,48,1536]{2,1,0:T(8,128)}, f32[2,48,1536]{2,1,0:T(8,128)}, u32[]{:S(2)}, u32[]{:S(2)}) collective-permute-start(f32[2,48,1536]{2,1,0:T(8,128)} %shard_map.235.refs_2_.refs_5_), channel_id=1, source_target_pairs={{0,2},{2,0},{4,6},{6,4},{8,10},{10,8},{12,14},{14,12},{16,18},{18,... | collective-permute-start | bytes 1769480 | tf_op jit(solution)/shard_map/ppermute | solution.py:91
  170.0 31.2 %collective-permute-start.29 = (f32[2,384,768]{2,1,0:T(8,128)S(1)}, f32[2,384,768]{2,1,0:T(8,128)S(1)}, u32[]{:S(2)}, u32[]{:S(2)}) collective-permute-start(f32[2,384,768]{2,1,0:T(8,128)S(1)} %shard_map.263.refs_3_), channel_id=1, source_target_pairs={{0,2},{2,0},{4,6},{6,4},{8,10},{10,8},{12,14},{14,12},{16,18},{18,... | collective-permute-start | bytes 7077896 | tf_op jit(solution)/shard_map/ppermute | solution.py:91
  170.2 28.3 %collective-permute-start.30 = (f32[1,384,768]{2,1,0:T(8,128)S(1)}, f32[1,384,768]{2,1,0:T(8,128)S(1)}, u32[]{:S(2)}, u32[]{:S(2)}) collective-permute-start(f32[1,384,768]{2,1,0:T(8,128)S(1)} %shard_map.259.refs_5_), channel_id=1, source_target_pairs={{0,1},{1,0},{2,3},{3,2},{4,5},{5,4},{6,7},{7,6},{8,9},{9,8},{10,11... | collective-permute-start | bytes 3538952 | tf_op jit(solution)/shard_map/ppermute | solution.py:95
  175.5 27.4 %collective-permute-start.28 = (f32[2,384,384]{2,1,0:T(8,128)S(1)}, f32[2,384,384]{2,1,0:T(8,128)S(1)}, u32[]{:S(2)}, u32[]{:S(2)}) collective-permute-start(f32[2,384,384]{2,1,0:T(8,128)S(1)} %shard_map.266.refs_3_), channel_id=1, source_target_pairs={{0,2},{2,0},{4,6},{6,4},{8,10},{10,8},{12,14},{14,12},{16,18},{18,... | collective-permute-start | bytes 3538952 | tf_op jit(solution)/shard_map/ppermute | solution.py:91
  175.7 48.1 %collective-permute-start.34 = (f32[2,192,768]{2,1,0:T(8,128)S(1)}, f32[2,192,768]{2,1,0:T(8,128)S(1)}, u32[]{:S(2)}, u32[]{:S(2)}) collective-permute-start(f32[2,192,768]{2,1,0:T(8,128)S(1)} %get-tuple-element.110.refs_3_), channel_id=1, source_target_pairs={{0,4},{2,6},{4,0},{6,2},{8,12},{10,14},{12,8},{14,10},{16,20},{18,... | collective-permute-start | bytes 3538952 | tf_op jit(solution)/shard_map/ppermute | solution.py:91
  199.6 24.4 %collective-permute-start.33 = (f32[1,192,768]{2,1,0:T(8,128)S(1)}, f32[1,192,768]{2,1,0:T(8,128)S(1)}, u32[]{:S(2)}, u32[]{:S(2)}) collective-permute-start(f32[1,192,768]{2,1,0:T(8,128)S(1)} %get-tuple-element.114.refs_4_), channel_id=1, source_target_pairs={{0,4},{2,6},{4,0},{6,2},{8,12},{10,14},{12,8},{14,10},{16,20},{18,... | collective-permute-start | bytes 1769480 | tf_op jit(solution)/shard_map/ppermute | solution.py:91
  238.3 76.6 %collective-permute-start.41 = (f32[2,384,768]{2,1,0:T(8,128)S(1)}, f32[2,384,768]{2,1,0:T(8,128)S(1)}, u32[]{:S(2)}, u32[]{:S(2)}) collective-permute-start(f32[2,384,768]{2,1,0:T(8,128)S(1)} %shard_map.276.refs_3_), channel_id=1, source_target_pairs={{0,2},{2,0},{4,6},{6,4},{8,10},{10,8},{12,14},{14,12},{16,18},{18,... | collective-permute-start | bytes 7077896 | tf_op jit(solution)/shard_map/ppermute | solution.py:91
  238.4 28.8 %collective-permute-start.37 = (f32[1,384,768]{2,1,0:T(8,128)S(1)}, f32[1,384,768]{2,1,0:T(8,128)S(1)}, u32[]{:S(2)}, u32[]{:S(2)}) collective-permute-start(f32[1,384,768]{2,1,0:T(8,128)S(1)} %shard_map.267.refs_4_), channel_id=1, source_target_pairs={{0,1},{1,0},{2,3},{3,2},{4,5},{5,4},{6,7},{7,6},{8,9},{9,8},{10,11... | collective-permute-start | bytes 3538952 | tf_op jit(solution)/shard_map/ppermute | solution.py:95
  240.0 73.5 %collective-permute-start.25 = (f32[512,768]{1,0:T(8,128)S(1)}, f32[512,768]{1,0:T(8,128)S(1)}, u32[]{:S(2)}, u32[]{:S(2)}) collective-permute-start(f32[512,768]{1,0:T(8,128)S(1)} %get-tuple-element.99), channel_id=1, source_target_pairs={{0,1},{1,0},{2,3},{3,2},{4,5},{5,4},{6,7},{7,6},{8,9},{9,8},{10,11... | collective-permute-start | bytes 4718600 | tf_op jit(solution)/shard_map/ppermute | solution.py:95
  256.7 56.4 %collective-permute-start.32 = (f32[1,384,384]{2,1,0:T(8,128)S(1)}, f32[1,384,384]{2,1,0:T(8,128)S(1)}, u32[]{:S(2)}, u32[]{:S(2)}) collective-permute-start(f32[1,384,384]{2,1,0:T(8,128)S(1)} %shard_map.270.refs_6_), channel_id=1, source_target_pairs={{0,1},{1,0},{2,3},{3,2},{4,5},{5,4},{6,7},{7,6},{8,9},{9,8},{10,11... | collective-permute-start | bytes 1769480 | tf_op jit(solution)/shard_map/ppermute | solution.py:95
  261.9 57.4 %collective-permute-start.40 = (f32[2,384,384]{2,1,0:T(8,128)S(1)}, f32[2,384,384]{2,1,0:T(8,128)S(1)}, u32[]{:S(2)}, u32[]{:S(2)}) collective-permute-start(f32[2,384,384]{2,1,0:T(8,128)S(1)} %shard_map.277.refs_4_), channel_id=1, source_target_pairs={{0,2},{2,0},{4,6},{6,4},{8,10},{10,8},{12,14},{14,12},{16,18},{18,... | collective-permute-start | bytes 3538952 | tf_op jit(solution)/shard_map/ppermute | solution.py:91
  267.2 52.7 %collective-permute-start.44 = (f32[2,192,768]{2,1,0:T(8,128)S(1)}, f32[2,192,768]{2,1,0:T(8,128)S(1)}, u32[]{:S(2)}, u32[]{:S(2)}) collective-permute-start(f32[2,192,768]{2,1,0:T(8,128)S(1)} %get-tuple-element.115.refs_3_), channel_id=1, source_target_pairs={{0,4},{2,6},{4,0},{6,2},{8,12},{10,14},{12,8},{14,10},{16,20},{18,... | collective-permute-start | bytes 3538952 | tf_op jit(solution)/shard_map/ppermute | solution.py:91
  317.3 36.9 %collective-permute-start.43 = (f32[1,384,768]{2,1,0:T(8,128)S(1)}, f32[1,384,768]{2,1,0:T(8,128)S(1)}, u32[]{:S(2)}, u32[]{:S(2)}) collective-permute-start(f32[1,384,768]{2,1,0:T(8,128)S(1)} %shard_map.283.refs_4_), channel_id=1, source_target_pairs={{0,1},{1,0},{2,3},{3,2},{4,5},{5,4},{6,7},{7,6},{8,9},{9,8},{10,11... | collective-permute-start | bytes 3538952 | tf_op jit(solution)/shard_map/ppermute | solution.py:95
  320.1 31.9 %collective-permute-start.45 = (f32[2,96,768]{2,1,0:T(8,128)S(1)}, f32[2,96,768]{2,1,0:T(8,128)S(1)}, u32[]{:S(2)}, u32[]{:S(2)}) collective-permute-start(f32[2,96,768]{2,1,0:T(8,128)S(1)} %get-tuple-element.147.refs_2_), channel_id=1, source_target_pairs={{0,8},{2,10},{4,12},{6,14},{8,0},{10,2},{12,4},{14,6},{16,24},{18,... | collective-permute-start | bytes 1769480 | tf_op jit(solution)/shard_map/ppermute | solution.py:91
  369.2 55.3 %collective-permute-start.38 = (f32[512,768]{1,0:T(8,128)}, f32[512,768]{1,0:T(8,128)}, u32[]{:S(2)}, u32[]{:S(2)}) collective-permute-start(f32[512,768]{1,0:T(8,128)} %get-tuple-element.136.refs_6_.refs_1_), channel_id=1, source_target_pairs={{0,1},{1,0},{2,3},{3,2},{4,5},{5,4},{6,7},{7,6},{8,9},{9,8},{10,11... | collective-permute-start | bytes 4718600 | tf_op jit(solution)/shard_map/ppermute | solution.py:95
  384.2 22.5 %collective-permute-start.60 = (f32[1,48,768]{2,1,0:T(8,128)S(1)}, f32[1,48,768]{2,1,0:T(8,128)S(1)}, u32[]{:S(2)}, u32[]{:S(2)}) collective-permute-start(f32[1,48,768]{2,1,0:T(8,128)S(1)} %get-tuple-element.205), channel_id=1, source_target_pairs={{0,1},{1,0},{2,3},{3,2},{4,5},{5,4},{6,7},{7,6},{8,9},{9,8},{10,11... | collective-permute-start | bytes 442376 | tf_op jit(solution)/shard_map/ppermute | solution.py:95
  385.7 24.2 %collective-permute-start.58 = (f32[2,48,384]{2,1,0:T(8,128)S(1)}, f32[2,48,384]{2,1,0:T(8,128)S(1)}, u32[]{:S(2)}, u32[]{:S(2)}) collective-permute-start(f32[2,48,384]{2,1,0:T(8,128)S(1)} %get-tuple-element.165.refs_2_), channel_id=1, source_target_pairs={{0,16},{2,18},{4,20},{6,22},{8,24},{10,26},{12,28},{14,30},{16,0},... | collective-permute-start | bytes 442376 | tf_op jit(solution)/shard_map/ppermute | solution.py:91
  (98 other events, 949.0 us)
